TPU v7x, 128 devices: a whole 4x4x4 slice. The times are simulated.
128 devices in a mesh: tm: 128 (over z, x, y, core).
Axes of the slice: x: 4, y: 4, z: 4, core: 2. Of those that a mesh axis runs over, the one named last changes fastest.
Arguments:
- transitions: float32 [1024, 256, 256], P('tm'), may hold values from -1 to 1
- noise_factor: float32 [1024, 256, 256], P('tm'), may hold values from -1 to 1, as said below
- forcing: float32 [1024, 256], P('tm'), may hold values from -0.3125 to 0.3125
- initial_mean: float32 [256], replicated, may hold values from -6 to 6
- initial_factor: float32 [256, 256], replicated, may hold values from -2 to 2, as said below
Outputs:
- means: float32 [1024, 256], P('tm')
- factors: float32 [1024, 256, 256], P('tm')
- log_scale: float32 [], replicated
Inputs may be any that keep to these rules, and one draw needn't show every extreme that they name: `noise_factor`: each matrix is lower triangular with a positive diagonal. `initial_factor`: lower triangular with a positive diagonal.
All inputs are finite; a program needn't handle non-finite values.
Results may differ from a plain program's by a relative error of at most 0.0003.
Values sent between devices are 32-bit elements; how exact they have to be, the bound alone decides.
No kernel may reach another device: no remote copies, remote signals or barrier semaphores. Data moves between devices by JAX's collectives and lax.ppermute only.
A program may use at most 192 MiB of HBM per device.

v0:
```python
import jax
import jax.numpy as jnp
from jax import lax
from jax.sharding import PartitionSpec as P

highest = lax.Precision.HIGHEST


def prefix(value, axis, join, neutral):
    count, mine = (lax.axis_size(axis), lax.axis_index(axis))
    pieces = jax.tree.map(lambda part: lax.all_gather(part, axis), value)
    running = jax.tree.map(
        lambda part, zero: jnp.full_like(part, 0) + jnp.asarray(zero, part.dtype), value, neutral
    )

    def step(position, running):
        longer = join(running, jax.tree.map(lambda part: part[position], pieces))
        return jax.tree.map(lambda new, old: jnp.where(position < mine, new, old), longer, running)

    return lax.fori_loop(0, count - 1, step, running)


def matmul(left, right):
    return jnp.einsum("...ij,...jk->...ik", left, right, precision=highest)


def matvec(left, right):
    return jnp.einsum("...ij,...j->...i", left, right, precision=highest)


def flipped(matrix):
    return jnp.swapaxes(matrix, -1, -2)


def combine(earlier, later):
    trans_one, offset_one, cov_one = earlier
    trans_two, offset_two, cov_two = later
    trans = matmul(trans_two, trans_one)
    offset = matvec(trans_two, offset_one) + offset_two
    cov = matmul(matmul(trans_two, cov_one), flipped(trans_two)) + cov_two
    return (trans, offset, cov)


def identity_element(width):
    return (
        jnp.eye(width, dtype=jnp.float32),
        jnp.zeros((width,), jnp.float32),
        jnp.zeros((width, width), jnp.float32),
    )


def local_prefix(elements, width):

    def advance(carry, step):
        merged = combine(carry, step)
        return (merged, merged)

    final_state, stacked = lax.scan(advance, identity_element(width), elements)
    return (final_state, stacked)


def earlier_blocks(total, width):
    return prefix(total, "tm", combine, identity_element(width))


def on_device(transitions, noise_factor, forcing, initial_mean, initial_factor):
    width = transitions.shape[1]
    noise_cov = matmul(noise_factor, flipped(noise_factor))
    elements = (transitions, forcing, noise_cov)
    start_cov = matmul(initial_factor, flipped(initial_factor))
    total, stacked = local_prefix(elements, width)
    prior = earlier_blocks(total, width)
    trans_in, offset_in, cov_in = prior
    mean_in = matvec(trans_in, initial_mean) + offset_in
    state_cov = matmul(matmul(trans_in, start_cov), flipped(trans_in)) + cov_in
    mean_in, state_cov = (mean_in, state_cov)
    trans_pre, offset_pre, cov_pre = stacked
    means = matvec(trans_pre, mean_in) + offset_pre
    covs = matmul(matmul(trans_pre, state_cov), flipped(trans_pre)) + cov_pre
    factors = jnp.linalg.cholesky(covs)
    local_logs = jnp.sum(jnp.log(jnp.diagonal(factors, axis1=1, axis2=2)))
    summed = lax.psum(local_logs, "tm")
    log_scale = summed / (lax.axis_size("tm") * transitions.shape[0] * width)
    return (means, factors, log_scale)


def solution(mesh):
    placed = (P("tm", None, None), P("tm", None, None), P("tm", None), P(), P())
    return jax.shard_map(
        on_device,
        mesh=mesh,
        in_specs=placed,
        out_specs=(P("tm", None), P("tm", None, None), P()),
        check_vma=False,
    )
```

profile of v0, /device:TPU:0, one launch (start us, length us, event | category | flops | bytes accessed | tf_op | source)
XLA Modules:
  0.0 1467.0 jit_solution(6813487538984108989)
XLA Ops:
  8.8 3.5 fusion.44
  12.4 56.5 %while.39 = (s32[]{:T(128)}, f32[256,256]{1,0:T(8,128)S(1)}, f32[256]{0:T(256)S(1)}, f32[256,256]{1,0:T(8,128)S(1)}, f32[8,256,256]{2,1,0:T(8,128)S(1)}, /*index...) while((s32[]{:T(128)}, f32[256,256]{1,0:T(8,128)S(1)}, ...), condition=%wide.region_1.2_spmd.clone, body=%wide.region_0.1_spmd.clone.sunk | while | flops 604897792 | bytes 4733576 | solution.py:58
  70.4 37.6 %all-gather.3 = f32[128,1,256]{2,1,0:T(1,128)S(1)} all-gather(f32[1,1,256]{2,1,0:T(1,128)S(1)} %bitcast.140), channel_id=3, replica_groups=mesh['tm'=128] {'tm'}, dimensions={0}, use_global_device_ids=true | all-gather | bytes 132096 | tf_op jit(solution)/shard_map/all_gather | solution.py:11
  109.2 69.8 %all-gather.7.cloned.1.call-done = f32[32768,256]{1,0:T(8,128)} async-done(((f32[256,256]{1,0:T(8,128)}), f32[32768,256]{1,0:T(8,128)}) %all-gather.7.cloned.1.call-update) | async-done | bytes 33554448 | tf_op jit(solution)/shard_map/all_gather | solution.py:11
  179.0 109.1 %all-gather.9.cloned.1.call-done = f32[32768,256]{1,0:T(8,128)} async-done(((f32[256,256]{1,0:T(8,128)}), f32[32768,256]{1,0:T(8,128)}) %all-gather.9.cloned.1.call-update) | async-done | bytes 33554448 | tf_op jit(solution)/shard_map/all_gather | solution.py:11
  288.1 792.5 %while.40 = (s32[]{:T(128)}, f32[256,256]{1,0:T(8,128)S(1)}, f32[256]{0:T(256)S(1)}, f32[256,256]{1,0:T(8,128)S(1)}, s32[]{:T(128)}, /*index=5*/f32[128,256,256]...) while((s32[]{:T(128)}, f32[256,256]{1,0:T(8,128)S(1)}, ...), condition=%wide.region_3.4_spmd.clone, body=%wide.region_2.3_spmd.clone.sunk | while | flops 605094912 | bytes 3945090 | solution.py:20
  295.7 1.5 fusion.113
  301.9 1.5 fusion.113
  308.2 1.5 fusion.113
  314.4 1.5 fusion.113
  320.7 1.5 fusion.113
  326.9 1.5 fusion.113
  333.1 1.5 fusion.113
  339.4 1.5 fusion.113
  345.6 1.5 fusion.113
  351.9 1.5 fusion.113
  358.1 1.5 fusion.113
  364.3 1.5 fusion.113
  370.6 1.5 fusion.113
  376.8 1.5 fusion.113
  383.1 1.5 fusion.113
  389.3 1.5 fusion.113
  395.5 1.5 fusion.113
  401.8 1.5 fusion.113
  408.0 1.5 fusion.113
  414.3 1.5 fusion.113
  420.5 1.5 fusion.113
  426.7 1.5 fusion.113
  433.0 1.5 fusion.113
  439.2 1.5 fusion.113
  445.5 1.5 fusion.113
  451.7 1.5 fusion.113
  457.9 1.5 fusion.113
  464.2 1.5 fusion.113
  470.4 1.5 fusion.113
  476.7 1.5 fusion.113
  482.9 1.5 fusion.113
  489.1 1.5 fusion.113
  495.4 1.5 fusion.113
  501.6 1.5 fusion.113
  507.9 1.5 fusion.113
  514.1 1.5 fusion.113
  520.3 1.5 fusion.113
  526.6 1.5 fusion.113
  532.8 1.5 fusion.113
  539.1 1.5 fusion.113
  545.3 1.5 fusion.113
  551.5 1.5 fusion.113
  557.8 1.5 fusion.113
  564.0 1.5 fusion.113
  1081.4 1.9 fusion.49
  1083.3 3.6 convolution_add_fusion.2
  1086.9 3.1 copy.28
  1090.0 1.9 fusion.38
  1093.3 93.8 %custom-call.13 = f32[8,128,128]{2,1,0:T(8,128)S(1)} custom-call(f32[8,128,128]{2,1,0:T(8,128)S(1)} %cholesky.119), custom_call_target="Cholesky" | custom-call | tf_op jit(solution)/shard_map/jit(cholesky)/cholesky | solution.py:80
  1187.3 79.5 %custom-call.14 = f32[8,1,128,128]{2,3,1,0:T(8,128)} custom-call(f32[8,1,128,128]{3,2,1,0:T(8,128)S(1)} %select_bitcast_fusion), custom_call_target="InvertDiagBlocksLowerTriangular" | custom-call | tf_op jit(solution)/shard_map/jit(cholesky)/cholesky | solution.py:80
  1266.8 1.8 constant_dynamic-update-slice_fusion.2
  1268.6 3.1 convolution_subtract_fusion
  1271.7 94.6 %custom-call.15 = f32[8,128,128]{2,1,0:T(8,128)S(1)} custom-call(f32[8,128,128]{2,1,0:T(8,128)} %convolution_subtract_fusion), custom_call_target="Cholesky" | custom-call | tf_op jit(solution)/shard_map/jit(cholesky)/cholesky | solution.py:80
  1366.5 1.6 select_select_fusion
  1368.1 17.8 %copy.31 = f32[8,256,256]{0,2,1:T(8,128)} copy(f32[8,256,256]{2,1,0:T(8,128)} %select_select_fusion) | data formatting | bytes 4194304 | tf_op jit(solution)/shard_map/jit(cholesky)/select_n | solution.py:80
  1386.0 2.3 gather_fusion
  1388.9 65.1 %psum.7 = f32[]{:T(128)} all-reduce(f32[]{:T(128)} %log_reduce_fusion), channel_id=1, replica_groups=mesh['tm'=128] {'tm'}, use_global_device_ids=true, to_apply=%region_9.10 | all-reduce | flops 1 | bytes 8 | tf_op jit(solution)/shard_map/psum | solution.py:82
  1454.3 3.5 fusion.46
  (1111 shorter events, 783.9 us)
Async XLA Ops:
  7.2 1.6 copy-start
  7.2 171.8 %all-gather.7.cloned.1.call-start = ((), (), s32[]{:S(2)}) async-start(), calls=%async_computation | async-start | bytes 33816576 | tf_op jit(solution)/shard_map/all_gather | solution.py:11
  12.4 96.4 %copy-start.8 = (f32[256,256]{1,0:T(8,128)S(1)}, f32[256,256]{1,0:T(8,128)}, u32[]{:S(2)}) copy-start(f32[256,256]{1,0:T(8,128)} %param.13) | copy-start | bytes 786436
  68.9 0.7 copy-start.5
  68.9 0.8 copy-start.3
  68.9 1014.4 %copy-start.2 = (f32[8,256,256]{2,1,0:T(8,128)}, f32[8,256,256]{2,1,0:T(8,128)S(1)}, u32[]{:S(2)}) copy-start(f32[8,256,256]{2,1,0:T(8,128)S(1)} %get-tuple-element.201) | copy-start | bytes 6291460
  69.7 218.5 %all-gather.9.cloned.1.call-start = ((), (), s32[]{:S(2)}) async-start(), calls=%async_computation.1 | async-start | bytes 33816576 | tf_op jit(solution)/shard_map/all_gather | solution.py:11
  1081.4 1.9 copy-start.7
  1086.9 3.1 copy-start.4
  1091.9 1.3 copy-start.6
  1368.1 85.9 %copy-start.9 = (f32[256]{0:T(256)S(1)}, f32[256]{0:T(256)}, u32[]{:S(2)}) copy-start(f32[256]{0:T(256)} %param.12) | copy-start | bytes 3076
  1368.1 90.9 %copy-start.1 = (f32[8,256,256]{2,1,0:T(8,128)S(1)}, f32[8,256,256]{2,1,0:T(8,128)}, u32[]{:S(2)}) copy-start(f32[8,256,256]{2,1,0:T(8,128)} %param.10) | copy-start | bytes 6291460
Sparse Core Ops, SparseCore 0:
  69.8 109.1 all-gather.6
  182.0 106.0 all-gather.8
where the time goes:
time: 1490 us; the launch traced here: 1470 us
  matrix products  745 us (50%)
  other arithmetic  275 us (18%)
  waiting for transfers between devices  180 us (12%)
  local copies, waits for them, and re-layouts  140 us (9%)
  blocking collectives  103 us (7%)
  between operations  16.1 us (1%)
    dot_general x411, matrix products, matmul(): return jnp.einsum('...ij,...jk->...ik', left, right, precision=highest)  572 us
    another operation x9, other arithmetic, on_device(): factors = jnp.linalg.cholesky(covs)  268 us
    all_gather x2, waiting for transfers between devices, prefix(): pieces = jax.tree.map(lambda part: lax.all_gather(part, axis), value)  179 us
    dot_general x137, matrix products, matvec(): return jnp.einsum('...ij,...j->...i', left, right, precision=highest)  169 us
    dynamic_slice x127, local copies, waits for them, and re-layouts, step(): longer = join(running, jax.tree.map(lambda part: part[position], pieces))  96.7 us
    psum x1, blocking collectives, on_device(): summed = lax.psum(local_logs, 'tm')  65.1 us
    all_gather x1, blocking collectives, prefix(): pieces = jax.tree.map(lambda part: lax.all_gather(part, axis), value)  37.6 us
  transfers between devices with their start and end apart: 2, of which 2 were waited for; matrix products, arithmetic and copies ran while one was open for 0% of the time, Pallas kernels for 0%

commit v1 on v0

v1 whole, which is shorter than its diff:
```python
import jax
import jax.numpy as jnp
from jax import lax
from jax.experimental import pallas as pl
from jax.experimental.pallas import tpu as pltpu
from jax.sharding import Mesh, PartitionSpec as P

f32, bf16 = jnp.float32, jnp.bfloat16
AXES = ("z", "x", "y", "c")
N = 256
H = 128
STEPS = 8
ROWS = 400
HALF = ROWS // 2
PB = 8


def split(x):
    hi = x.astype(bf16)
    return hi, (x - hi.astype(f32)).astype(bf16)


def dg(a, b, ca, cb):
    return lax.dot_general(a, b, (((ca,), (cb,)), ((), ())), preferred_element_type=f32)


def mm3(a, b, ca=1, cb=0):
    return dg(a[0], b[0], ca, cb) + (dg(a[0], b[1], ca, cb) + dg(a[1], b[0], ca, cb))


def row_times(vec, a):
    v1 = vec.astype(bf16)
    rest = vec - v1.astype(f32)
    v2 = rest.astype(bf16)
    v3 = (rest - v2.astype(f32)).astype(bf16)
    out = dg(v3, a[0], 1, 1) + dg(v2, a[1], 1, 1)
    out = out + (dg(v2, a[0], 1, 1) + dg(v1, a[1], 1, 1))
    return out + dg(v1, a[0], 1, 1)


def grid_iota():
    return (
        lax.broadcasted_iota(jnp.int32, (H, H), 0),
        lax.broadcasted_iota(jnp.int32, (H, H), 1),
    )


def pack(out, a, p, b):
    r, c = grid_iota()
    out[0:N, :] = a
    out[N : N + H, 0:H] = p[H:, :H]
    out[N : N + H, H:] = jnp.where(r >= c, p[:H, :H], p[H:, H:])
    diag = jnp.sum(jnp.where(r == c, p[H:, H:], 0.0), axis=0, keepdims=True)
    row = lax.broadcasted_iota(jnp.int32, (8, N), 0)
    wide = jnp.concatenate([diag, diag], axis=1)
    out[N + H : N + H + 8, :] = jnp.where(row == 0, b, jnp.broadcast_to(wide, (8, N)))
    out[N + H + 8 :, :] = jnp.zeros((8, N), f32)


def unpack(ref):
    r, c = grid_iota()
    a = ref[0:N, :]
    x = ref[N : N + H, H:]
    tail = ref[N + H : N + H + 8, :]
    d2 = tail[1:2, :H]
    z11 = jnp.where(r > c, x, jnp.where(r == c, 0.5 * x, 0.0))
    z22 = jnp.where(r < c, x, jnp.where(r == c, 0.5 * jnp.broadcast_to(d2, (H, H)), 0.0))
    top = jnp.concatenate([z11, jnp.zeros((H, H), f32)], axis=1)
    low = jnp.concatenate([ref[N : N + H, :H], z22], axis=1)
    return a, jnp.concatenate([top, low], axis=0), jnp.broadcast_to(tail[0:1, :], (8, N))


def compose(later, earlier):
    a2 = split(later[0])
    a1, z1 = split(earlier[0]), split(earlier[1])
    a = mm3(a2, a1)
    z = mm3(split(mm3(a2, z1)), a2, 1, 1) + later[1]
    return a, z, row_times(earlier[2], a2) + later[2]


def apply_to(element, state):
    a = split(element[0])
    z = mm3(split(mm3(a, split(state[0]))), a, 1, 1) + element[1]
    return z, row_times(state[1], a) + element[2]


def local_kernel(t_ref, n_ref, f_ref, a_out, p_out, b_out, total):
    a = p = b = None
    for k in range(STEPS):
        noise = split(n_ref[k])
        q = mm3(noise, noise, 1, 1)
        push = jnp.broadcast_to(f_ref[k : k + 1, :], (8, N))
        if k == 0:
            a, p, b = t_ref[0], q, push
        else:
            t = split(t_ref[k])
            a = mm3(t, split(a))
            p = mm3(split(mm3(t, split(p))), t, 1, 1) + q
            b = row_times(b, t) + push
        a_out[k] = a
        p_out[k] = p
        b_out[k] = b
    pack(total, a, p, b)


def take_half(half, whole, c):
    half[...] = whole[pl.ds(pl.multiple_of(c * HALF, 8), HALF), :]


def core_kernel(place, own, other, half, total):
    c = place[3]

    def join(earlier, later):
        a, z, b = compose(unpack(later), unpack(earlier))
        pack(total, a, z + z.T, b)

    @pl.when(c == 0)
    def _():
        join(own, other)

    @pl.when(c == 1)
    def _():
        join(other, own)

    take_half(half, total, c)


def ring_kernel(which, place, own, r1, r2, r3, s1, s2, s3, half, total, ea, ez, eb, pieces):
    me, c = place[which], place[3]
    here = pl.multiple_of(c * HALF, 8)
    there = pl.multiple_of((1 - c) * HALF, 8)
    pieces[me] = own[...]
    for back, r, s in ((1, r1, s1), (2, r2, s2), (3, r3, s3)):
        spot = lax.rem(me + 4 - back, 4)
        pieces[spot, pl.ds(here, HALF), :] = r[...]
        pieces[spot, pl.ds(there, HALF), :] = s[...]
    state = unpack(pieces.at[0])
    eye = (
        lax.broadcasted_iota(jnp.int32, (N, N), 0) == lax.broadcasted_iota(jnp.int32, (N, N), 1)
    )
    ea[...] = jnp.where(eye, 1.0, 0.0)
    ez[...] = jnp.zeros((N, N), f32)
    eb[...] = jnp.zeros((8, N), f32)
    for p in range(1, 4):

        @pl.when(me == p)
        def _():
            ea[...] = state[0]
            ez[...] = state[1]
            eb[...] = state[2]

        state = compose(unpack(pieces.at[p]), state)
    a, z, b = state
    pack(total, a, z + z.T, b)
    take_half(half, total, c)


def lane(x, i):
    return jnp.take_along_axis(
        x, jnp.full(x.shape, i, jnp.int32), axis=1, mode="promise_in_bounds"
    )


def factor(rows, n):
    width = len(rows)

    def panel(q, _):
        j0 = q * PB
        held = [[ref[pl.ds((j0 + t) * 8, 8), :] for t in range(PB)] for ref in rows]
        for t in range(PB):
            inv = lax.rsqrt(lane(held[0][t], j0 + t))
            for w in range(width):
                held[w][t] = held[w][t] * inv
            for s in range(t + 1, PB):
                c = lane(held[0][t], j0 + s)
                for w in range(width):
                    held[w][s] = held[w][s] - c * held[w][t]
        for w in range(width):
            for t in range(PB):
                rows[w][pl.ds((j0 + t) * 8, 8), :] = held[w][t]

        def trail(p, _):
            i0 = p * PB
            for s in range(PB):
                acc = [rows[w][pl.ds((i0 + s) * 8, 8), :] for w in range(width)]
                for t in range(PB):
                    c = lane(held[0][t], i0 + s)
                    for w in range(width):
                        acc[w] = acc[w] - c * held[w][t]
                for w in range(width):
                    rows[w][pl.ds((i0 + s) * 8, 8), :] = acc[w]
            return 0

        lax.fori_loop(q + 1, n // PB, trail, 0)
        return 0

    lax.fori_loop(0, n // PB, panel, 0)


def strided(m):
    return pl.ds(m, H, stride=STEPS)


def cholesky(cov, l_ref, logs_ref, d1, b1, d2):
    for m in range(STEPS):
        d1[strided(m), :] = cov[m, 0:H, 0:H]
        b1[strided(m), :] = cov[m, 0:H, H:]
    factor([d1, b1], H)
    for m in range(STEPS):
        u = split(b1[strided(m), :])
        d2[strided(m), :] = cov[m, H:, H:] - mm3(u, u, 0, 0)
    factor([d2], H)
    r, c = grid_iota()
    total = jnp.zeros((1, H), f32)
    for m in range(STEPS):
        u1 = d1[strided(m), :]
        u2 = d2[strided(m), :]
        logs = jnp.log(jnp.where(r == c, u1, 1.0)) + jnp.log(jnp.where(r == c, u2, 1.0))
        total = total + jnp.sum(logs, axis=0, keepdims=True)
        l_ref[m, 0:H, 0:H] = jnp.where(r <= c, u1, 0.0).T
        l_ref[m, H:, 0:H] = b1[strided(m), :].T
        l_ref[m, H:, H:] = jnp.where(r <= c, u2, 0.0).T
        l_ref[m, 0:H, H:] = jnp.zeros((H, H), f32)
    logs_ref[...] = jnp.broadcast_to(total, (8, H))


def final_kernel(place, r1, r2, r3, s1, s2, s3, xa, xz, xb, ya, yz, yb, core, a_ref, p_ref, b_ref, m0_ref, l0_ref,
                 means, l_ref, logs, pieces, zs, ms, cov, d1, b1, d2):
    me, c = place[0], place[3]
    here = pl.multiple_of(c * HALF, 8)
    there = pl.multiple_of((1 - c) * HALF, 8)
    for back, r, s in ((1, r1, s1), (2, r2, s2), (3, r3, s3)):
        spot = lax.rem(me + 4 - back, 4)
        pieces[spot, pl.ds(here, HALF), :] = r[...]
        pieces[spot, pl.ds(there, HALF), :] = s[...]
    l0 = split(l0_ref[...])
    zs[...] = 0.5 * mm3(l0, l0, 1, 1)
    ms[...] = jnp.broadcast_to(m0_ref[...], (8, N))

    def slab(k, _):
        zs[...], ms[...] = apply_to(unpack(pieces.at[k]), (zs[...], ms[...]))
        return 0

    lax.fori_loop(0, me, slab, 0)
    for ea, ez, eb in ((xa, xz, xb), (ya, yz, yb)):
        zs[...], ms[...] = apply_to((ea[...], ez[...], eb[...]), (zs[...], ms[...]))

    @pl.when(c == 1)
    def _():
        zs[...], ms[...] = apply_to(unpack(core), (zs[...], ms[...]))

    z = zs[...]
    state = split(z + z.T)
    mean = ms[...]
    for k in range(STEPS):
        a = split(a_ref[k])
        cov[k] = mm3(split(mm3(a, state)), a, 1, 1) + p_ref[k]
        means[k : k + 1, :] = (row_times(mean, a) + b_ref[k])[0:1, :]
    cholesky(cov, l_ref, logs, d1, b1, d2)


VMEM = pl.BlockSpec(memory_space=pltpu.VMEM)
SMEM = pl.BlockSpec(memory_space=pltpu.SMEM)


def shape(*dims):
    return jax.ShapeDtypeStruct(dims, f32)


def call(kernel, outs, specs, scratch, name):
    return pl.pallas_call(
        kernel,
        out_shape=outs,
        in_specs=specs,
        out_specs=(VMEM,) * len(outs),
        scratch_shapes=scratch,
        compiler_params=pltpu.CompilerParams(vmem_limit_bytes=48 * 2**20),
        name=name,
    )


def ring(axis, back):
    stride, count = {"c": (1, 2), "y": (2, 4), "x": (8, 4), "z": (32, 4)}[axis]
    pairs = []
    for i in range(128):
        p = (i // stride) % count
        pairs.append((i, i + ((p + back) % count - p) * stride))
    return pairs


def send(x, axis, back):
    return lax.ppermute(x, AXES, ring(axis, back))


def gather_ring(half, axis):
    got = [send(half, axis, back) for back in (1, 2, 3)]
    return got + [send(g, "c", 1) for g in got]


def on_device(transitions, noise_factor, forcing, initial_mean, initial_factor):
    place = jnp.stack([lax.axis_index(axis) for axis in AXES]).astype(jnp.int32)
    stack = shape(STEPS, N, N)
    packed, half = shape(ROWS, N), shape(HALF, N)
    element = (shape(N, N), shape(N, N), shape(8, N))
    a, p, b, own = call(
        local_kernel, (stack, stack, shape(STEPS, 8, N), packed), [VMEM] * 3, [], "local"
    )(transitions, noise_factor, forcing)
    other = send(own, "c", 1)
    mine, total = call(core_kernel, (half, packed), [SMEM, VMEM, VMEM], [], "core")(place, own, other)
    before = []
    for axis, which in (("y", 2), ("x", 1)):
        mine, total, *earlier = call(
            lambda *refs, which=which: ring_kernel(which, *refs),
            (half, packed) + element,
            [SMEM] + [VMEM] * 7,
            [pltpu.VMEM((4, ROWS, N), f32)],
            "ring_" + axis,
        )(place, total, *gather_ring(mine, axis))
        before.append(earlier)
    by_y, by_x = before
    means, factors, logs = call(
        final_kernel,
        (shape(STEPS, N), stack, shape(8, H)),
        [SMEM] + [VMEM] * 18,
        [
            pltpu.VMEM((4, ROWS, N), f32),
            pltpu.VMEM((N, N), f32),
            pltpu.VMEM((8, N), f32),
            pltpu.VMEM((STEPS, N, N), f32),
            pltpu.VMEM((STEPS * H, H), f32),
            pltpu.VMEM((STEPS * H, H), f32),
            pltpu.VMEM((STEPS * H, H), f32),
        ],
        "final",
    )(place, *gather_ring(mine, "z"), *by_x, *by_y, other, a, p, b, initial_mean[None], initial_factor)
    logs = logs + send(logs, "c", 1)
    for axis in ("y", "x", "z"):
        one, two, three = [send(logs, axis, k) for k in (1, 2, 3)]
        logs = (logs + two) + (one + three)
    log_scale = jnp.sum(logs[0]) / (128 * STEPS * N)
    return means, factors, log_scale


def solution(mesh):
    cube = Mesh(mesh.devices.reshape(4, 4, 4, 2), AXES)
    return jax.shard_map(
        on_device,
        mesh=cube,
        in_specs=(P(AXES, None, None), P(AXES, None, None), P(AXES, None), P(), P()),
        out_specs=(P(AXES, None), P(AXES, None, None), P()),
        check_vma=False,
    )
```

time: 1490 us -> 188 us (0.13); the launches traced: 1470 us -> 187 us
  matrix products: 745 us -> 0 us
  other arithmetic: 275 us -> 0.7 us
  local copies, waits for them, and re-layouts: 140 us -> 2.04 us
  waiting for transfers between devices: 180 us -> 52.3 us
  Pallas kernels: 0 us -> 104 us
  blocking collectives: 103 us -> 0 us
  starting transfers between devices: 0.08 us -> 25.7 us
    dot_general x548 -> x0, matrix products: 740 us -> none  [the longest x411 572 us: matmul(): return jnp.einsum('...ij,...jk->...ik', left, right, precision=highest)]
    another operation x10 -> x1, other arithmetic: 268 us -> 0.08 us  [on_device(): place = jnp.stack([lax.axis_index(axis) for axis in AXES]).astype(jnp.int32)]
    all_gather x2 -> x0, waiting for transfers between devices: 179 us -> none  [prefix(): pieces = jax.tree.map(lambda part: lax.all_gather(part, axis), value)]
    pallas_call x0 -> x5, Pallas kernels: none -> 104 us  [the longest x1 89.2 us: on_device(): call(final_kernel, (shape(STEPS, N), stack, shape(8, H)), [SMEM] + [VMEM]...]
    dynamic_slice x135 -> x0, local copies, waits for them, and re-layouts: 103 us -> none  [the longest x127 96.7 us: step(): longer = join(running, jax.tree.map(lambda part: part[position], pieces))]
    psum x1 -> x0, blocking collectives: 65.1 us -> none  [on_device(): summed = lax.psum(local_logs, 'tm')]
    ppermute x0 -> x29, waiting for transfers between devices: none -> 52.3 us  [send(): return lax.ppermute(x, AXES, ring(axis, back))]
    all_gather x1 -> x0, blocking collectives: 37.6 us -> none  [prefix(): pieces = jax.tree.map(lambda part: lax.all_gather(part, axis), value)]
  transfers between devices with their start and end apart: 2 -> 29, of which waited for: 2 -> 22; matrix products, arithmetic and copies ran while one was open for 0% -> 0% of each run, Pallas kernels for 0% -> 0%
where the time goes in v1:
time: 188 us; the launch traced here: 187 us
  Pallas kernels  104 us (55%)
  waiting for transfers between devices  52.3 us (28%)
  starting transfers between devices  25.7 us (14%)
  between operations  2.49 us (1%)
  local copies, waits for them, and re-layouts  2.04 us (1%)
    pallas_call x1, Pallas kernels, on_device(): call(final_kernel, (shape(STEPS, N), stack, shape(8, H)), [SMEM] + [VMEM]...  89.2 us
    ppermute x29, waiting for transfers between devices, send(): return lax.ppermute(x, AXES, ring(axis, back))  52.3 us
    ppermute x29, starting transfers between devices, send(): return lax.ppermute(x, AXES, ring(axis, back))  25.7 us
    pallas_call x1, Pallas kernels, on_device(): call(local_kernel, (stack, stack, shape(STEPS, 8, N), packed), [VMEM] * 3...  7.16 us
    pallas_call x2, Pallas kernels, on_device(): call(lambda *refs, which=which: ring_kernel(which, *refs), (half, packed)...  6.45 us
  transfers between devices with their start and end apart: 29, of which 22 were waited for; matrix products, arithmetic and copies ran while one was open for 0% of the time, Pallas kernels for 0%

profile of v1, /device:TPU:0, one launch (start us, length us, event | category | flops | bytes accessed | tf_op | source)
XLA Modules:
  0.0 187.3 jit_solution(4309186227778114358)
XLA Ops:
  0.6 0.7 copy-done.2
  1.3 7.2 %local.1 = (f32[8,256,256]{2,1,0:T(8,128)S(1)}, f32[8,256,256]{2,1,0:T(8,128)S(1)}, f32[8,8,256]{2,1,0:T(8,128)S(1)}, f32[400,256]{1,0:T(8,128)S(1)}) custom-call(f32[8,256,256]{2,1,0:T(8,128)} %t_ref.1, f32[8,256,256]{2,1,0:T(8,128)} %n_ref.1, f32[8,256]{1,0:T(8,128)S(1)} %copy-done.2), custom_call_target="tpu_custom_call" | custom-call | tf_op jit(solution)/shard_map/local/pallas_call | solution.py:305
  8.5 1.3 copy-done
  9.8 0.1 pad_add_fusion.place.refs_0_
  9.9 1.7 collective-permute-done.other.core
  11.6 1.3 core.1
  12.9 3.2 %collective-permute-start.3 = (f32[200,256]{1,0:T(8,128)S(1)}, f32[200,256]{1,0:T(8,128)S(1)}, u32[]{:S(2)}, u32[]{:S(2)}) collective-permute-start(f32[200,256]{1,0:T(8,128)S(1)} %get-tuple-element.23), channel_id=1, source_target_pairs={{0,6},{1,7},{2,0},{3,1},{4,2},{5,3},{6,4},{7,5},{8,14},{9,15},{10,... | collective-permute-start | bytes 614408 | tf_op jit(solution)/shard_map/ppermute | solution.py:292
  16.1 0.6 collective-permute-start.2
  16.7 1.0 collective-permute-start.1
  17.7 7.4 %collective-permute-done.3.refs_4_ = f32[200,256]{1,0:T(8,128)S(1)} collective-permute-done((f32[200,256]{1,0:T(8,128)S(1)}, f32[200,256]{1,0:T(8,128)S(1)}, u32[]{:S(2)}, u32[]{:S(2)}) %collective-permute-start.3) | collective-permute-done | bytes 204832 | tf_op jit(solution)/shard_map/ppermute | solution.py:292
  25.1 0.0 collective-permute-start.6
  25.1 0.5 collective-permute-done.2.refs_3_
  25.6 0.0 collective-permute-start.5
  25.6 3.2 %collective-permute-done.1.refs_2_ = f32[200,256]{1,0:T(8,128)S(1)} collective-permute-done((f32[200,256]{1,0:T(8,128)S(1)}, f32[200,256]{1,0:T(8,128)S(1)}, u32[]{:S(2)}, u32[]{:S(2)}) %collective-permute-start.1) | collective-permute-done | bytes 204832 | tf_op jit(solution)/shard_map/ppermute | solution.py:292
  28.8 0.0 collective-permute-start.4
  28.8 0.0 collective-permute-done.6.refs_7_
  28.8 1.4 collective-permute-done.4.refs_5_
  30.3 2.8 %ring_y.1 = (f32[200,256]{1,0:T(8,128)S(1)}, f32[400,256]{1,0:T(8,128)S(1)}, f32[256,256]{1,0:T(8,128)S(1)}, f32[256,256]{1,0:T(8,128)S(1)}, f32[8,256]{1,0:T(8,128)S(1)}) custom-call(s32[4]{0:T(128)S(1)} %pad_add_fusion.place.refs_0_, f32[400,256]{1,0:T(8,128)S(1)} %get-tuple-element.22.refs_1_, f32[200,256]{1,0:T(8,128)S(1)} %collective-permute-done.1.refs_2_, ...), custom_call_target="tpu_custom_call" | custom-call | tf_op jit(solution)/shard_map/ring_y/pallas_call | solution.py:312
  33.0 2.8 %collective-permute-start.9 = (f32[200,256]{1,0:T(8,128)S(1)}, f32[200,256]{1,0:T(8,128)S(1)}, u32[]{:S(2)}, u32[]{:S(2)}) collective-permute-start(f32[200,256]{1,0:T(8,128)S(1)} %get-tuple-element.25), channel_id=1, source_target_pairs={{0,24},{1,25},{2,26},{3,27},{4,28},{5,29},{6,30},{7,31},{8,0},{9,1... | collective-permute-start | bytes 614408 | tf_op jit(solution)/shard_map/ppermute | solution.py:292
  35.9 0.8 collective-permute-start.8
  36.7 0.9 collective-permute-start.7
  37.5 7.4 %collective-permute-done.9.refs_4_ = f32[200,256]{1,0:T(8,128)S(1)} collective-permute-done((f32[200,256]{1,0:T(8,128)S(1)}, f32[200,256]{1,0:T(8,128)S(1)}, u32[]{:S(2)}, u32[]{:S(2)}) %collective-permute-start.9) | collective-permute-done | bytes 204832 | tf_op jit(solution)/shard_map/ppermute | solution.py:292
  44.9 0.0 collective-permute-start.12
  44.9 0.4 collective-permute-done.8.refs_3_
  45.4 0.1 collective-permute-start.11
  45.4 3.2 %collective-permute-done.7.refs_2_ = f32[200,256]{1,0:T(8,128)S(1)} collective-permute-done((f32[200,256]{1,0:T(8,128)S(1)}, f32[200,256]{1,0:T(8,128)S(1)}, u32[]{:S(2)}, u32[]{:S(2)}) %collective-permute-start.7) | collective-permute-done | bytes 204832 | tf_op jit(solution)/shard_map/ppermute | solution.py:292
  48.6 0.0 collective-permute-start.10
  48.6 0.0 collective-permute-done.12.refs_7_
  48.6 1.4 collective-permute-done.10.refs_5_
  50.0 3.7 %ring_x.1 = (f32[200,256]{1,0:T(8,128)S(1)}, f32[400,256]{1,0:T(8,128)}, f32[256,256]{1,0:T(8,128)S(1)}, f32[256,256]{1,0:T(8,128)S(1)}, f32[8,256]{1,0:T(8,128)S(1)}) custom-call(s32[4]{0:T(128)S(1)} %pad_add_fusion.place.refs_0_, f32[400,256]{1,0:T(8,128)S(1)} %get-tuple-element.24.refs_1_, f32[200,256]{1,0:T(8,128)S(1)} %collective-permute-done.7.refs_2_, ...), custom_call_target="tpu_custom_call" | custom-call | tf_op jit(solution)/shard_map/ring_x/pallas_call | solution.py:312
  53.7 4.0 %collective-permute-start.15 = (f32[200,256]{1,0:T(8,128)S(1)}, f32[200,256]{1,0:T(8,128)S(1)}, u32[]{:S(2)}, u32[]{:S(2)}) collective-permute-start(f32[200,256]{1,0:T(8,128)S(1)} %get-tuple-element.26), channel_id=1, source_target_pairs={{0,96},{1,97},{2,98},{3,99},{4,100},{5,101},{6,102},{7,103},{8,104... | collective-permute-start | bytes 614408 | tf_op jit(solution)/shard_map/ppermute | solution.py:292
  57.8 0.0 collective-permute-start.14
  57.8 1.3 collective-permute-start.13
  59.0 7.8 %collective-permute-done.15.r3 = f32[200,256]{1,0:T(8,128)S(1)} collective-permute-done((f32[200,256]{1,0:T(8,128)S(1)}, f32[200,256]{1,0:T(8,128)S(1)}, u32[]{:S(2)}, u32[]{:S(2)}) %collective-permute-start.15) | collective-permute-done | bytes 204832 | tf_op jit(solution)/shard_map/ppermute | solution.py:292
  66.8 0.0 collective-permute-start.18
  66.8 0.4 collective-permute-done.14.r2
  67.2 0.1 collective-permute-start.17
  67.3 2.9 %collective-permute-done.13.r1 = f32[200,256]{1,0:T(8,128)S(1)} collective-permute-done((f32[200,256]{1,0:T(8,128)S(1)}, f32[200,256]{1,0:T(8,128)S(1)}, u32[]{:S(2)}, u32[]{:S(2)}) %collective-permute-start.13) | collective-permute-done | bytes 204832 | tf_op jit(solution)/shard_map/ppermute | solution.py:292
  70.2 0.0 collective-permute-start.16
  70.2 0.0 collective-permute-done.18.s3
  70.2 0.0 collective-permute-done.17.s2
  70.2 1.4 collective-permute-done.16.s1
  71.7 89.2 %final.1 = (f32[8,256]{1,0:T(8,128)}, f32[8,256,256]{2,1,0:T(8,128)}, f32[8,128]{1,0:T(8,128)S(1)}) custom-call(s32[4]{0:T(128)S(1)} %pad_add_fusion.place.refs_0_, f32[200,256]{1,0:T(8,128)S(1)} %collective-permute-done.13.r1, f32[200,256]{1,0:T(8,128)S(1)} %collective-permute-done.14.r2, f32[200,256]{1,0:T(8,128)S(1)} %collective-permute-done.15.r3, ...), custom_call_target="tpu_custom_call" | custom-call | tf_op jit(solution)/shard_map/final/pallas_call | solution.py:321
  160.8 0.8 collective-permute-start.19
  161.7 0.8 collective-permute-done.19
  162.5 0.7 collective-permute-start.22
  163.2 1.3 collective-permute-start.21
  164.5 0.6 collective-permute-start.20
  165.2 0.9 collective-permute-done.22
  166.1 1.9 %collective-permute-done.21 = f32[8,128]{1,0:T(8,128)S(1)} collective-permute-done((f32[8,128]{1,0:T(8,128)S(1)}, f32[8,128]{1,0:T(8,128)S(1)}, u32[]{:S(2)}, u32[]{:S(2)}) %collective-permute-start.21) | collective-permute-done | bytes 4128 | tf_op jit(solution)/shard_map/ppermute | solution.py:292
  168.0 1.6 collective-permute-done.20
  169.6 0.7 collective-permute-start.25
  170.3 1.4 collective-permute-start.24
  171.7 0.8 collective-permute-start.23
  172.5 0.8 collective-permute-done.25
  173.3 1.9 %collective-permute-done.24 = f32[8,128]{1,0:T(8,128)S(1)} collective-permute-done((f32[8,128]{1,0:T(8,128)S(1)}, f32[8,128]{1,0:T(8,128)S(1)}, u32[]{:S(2)}, u32[]{:S(2)}) %collective-permute-start.24) | collective-permute-done | bytes 4128 | tf_op jit(solution)/shard_map/ppermute | solution.py:292
  175.1 1.6 collective-permute-done.23
  176.8 3.0 %collective-permute-start.28 = (f32[8,128]{1,0:T(8,128)S(1)}, f32[8,128]{1,0:T(8,128)S(1)}, u32[]{:S(2)}, u32[]{:S(2)}) collective-permute-start(f32[8,128]{1,0:T(8,128)S(1)} %add_add_fusion.1), channel_id=1, source_target_pairs={{0,96},{1,97},{2,98},{3,99},{4,100},{5,101},{6,102},{7,103},{8,104... | collective-permute-start | bytes 12296 | tf_op jit(solution)/shard_map/ppermute | solution.py:292
  179.8 0.0 collective-permute-start.27
  179.8 1.5 collective-permute-start.26
  181.3 0.0 collective-permute-done.28
  181.3 3.3 %collective-permute-done.27 = f32[8,128]{1,0:T(8,128)S(1)} collective-permute-done((f32[8,128]{1,0:T(8,128)S(1)}, f32[8,128]{1,0:T(8,128)S(1)}, u32[]{:S(2)}, u32[]{:S(2)}) %collective-permute-start.27) | collective-permute-done | bytes 4128 | tf_op jit(solution)/shard_map/ppermute | solution.py:292
  184.6 0.3 collective-permute-done.26
  184.9 0.6 slice_reduce_fusion
  (13 shorter events, 0.0 us)
Async XLA Ops:
  0.6 0.7 copy-start.2
  8.5 1.3 copy-start
  9.8 61.8 %copy-start.1 = (f32[256,256]{1,0:T(8,128)S(1)}, f32[256,256]{1,0:T(8,128)}, u32[]{:S(2)}) copy-start(f32[256,256]{1,0:T(8,128)} %l0_ref.1) | copy-start | bytes 786436
  9.8 61.8 %copy-start.3 = (f32[256]{0:T(256)S(1)}, f32[256]{0:T(256)}, u32[]{:S(2)}) copy-start(f32[256]{0:T(256)} %param.8) | copy-start | bytes 3076
  9.8 1.7 collective-permute-start
  12.9 12.2 %collective-permute-start.3 = (f32[200,256]{1,0:T(8,128)S(1)}, f32[200,256]{1,0:T(8,128)S(1)}, u32[]{:S(2)}, u32[]{:S(2)}) collective-permute-start(f32[200,256]{1,0:T(8,128)S(1)} %get-tuple-element.23), channel_id=1, source_target_pairs={{0,6},{1,7},{2,0},{3,1},{4,2},{5,3},{6,4},{7,5},{8,14},{9,15},{10,... | collective-permute-start | bytes 614408 | tf_op jit(solution)/shard_map/ppermute | solution.py:292
  16.1 9.5 %collective-permute-start.2 = (f32[200,256]{1,0:T(8,128)S(1)}, f32[200,256]{1,0:T(8,128)S(1)}, u32[]{:S(2)}, u32[]{:S(2)}) collective-permute-start(f32[200,256]{1,0:T(8,128)S(1)} %get-tuple-element.23), channel_id=1, source_target_pairs={{0,4},{1,5},{2,6},{3,7},{4,0},{5,1},{6,2},{7,3},{8,12},{9,13},{10,... | collective-permute-start | bytes 614408 | tf_op jit(solution)/shard_map/ppermute | solution.py:292
  16.7 12.1 %collective-permute-start.1 = (f32[200,256]{1,0:T(8,128)S(1)}, f32[200,256]{1,0:T(8,128)S(1)}, u32[]{:S(2)}, u32[]{:S(2)}) collective-permute-start(f32[200,256]{1,0:T(8,128)S(1)} %get-tuple-element.23), channel_id=1, source_target_pairs={{0,2},{1,3},{2,4},{3,5},{4,6},{5,7},{6,0},{7,1},{8,10},{9,11},{10,... | collective-permute-start | bytes 614408 | tf_op jit(solution)/shard_map/ppermute | solution.py:292
  25.1 3.7 %collective-permute-start.6 = (f32[200,256]{1,0:T(8,128)S(1)}, f32[200,256]{1,0:T(8,128)S(1)}, u32[]{:S(2)}, u32[]{:S(2)}) collective-permute-start(f32[200,256]{1,0:T(8,128)S(1)} %collective-permute-done.3.refs_4_), channel_id=1, source_target_pairs={{0,1},{1,0},{2,3},{3,2},{4,5},{5,4},{6,7},{7,6},{8,9},{9,8},{10,11... | collective-permute-start | bytes 614408 | tf_op jit(solution)/shard_map/ppermute | solution.py:292
  25.6 3.2 %collective-permute-start.5 = (f32[200,256]{1,0:T(8,128)S(1)}, f32[200,256]{1,0:T(8,128)S(1)}, u32[]{:S(2)}, u32[]{:S(2)}) collective-permute-start(f32[200,256]{1,0:T(8,128)S(1)} %collective-permute-done.2.refs_3_), channel_id=1, source_target_pairs={{0,1},{1,0},{2,3},{3,2},{4,5},{5,4},{6,7},{7,6},{8,9},{9,8},{10,11... | collective-permute-start | bytes 614408 | tf_op jit(solution)/shard_map/ppermute | solution.py:292
  28.8 1.5 collective-permute-start.4
  33.0 11.9 %collective-permute-start.9 = (f32[200,256]{1,0:T(8,128)S(1)}, f32[200,256]{1,0:T(8,128)S(1)}, u32[]{:S(2)}, u32[]{:S(2)}) collective-permute-start(f32[200,256]{1,0:T(8,128)S(1)} %get-tuple-element.25), channel_id=1, source_target_pairs={{0,24},{1,25},{2,26},{3,27},{4,28},{5,29},{6,30},{7,31},{8,0},{9,1... | collective-permute-start | bytes 614408 | tf_op jit(solution)/shard_map/ppermute | solution.py:292
  35.9 9.5 %collective-permute-start.8 = (f32[200,256]{1,0:T(8,128)S(1)}, f32[200,256]{1,0:T(8,128)S(1)}, u32[]{:S(2)}, u32[]{:S(2)}) collective-permute-start(f32[200,256]{1,0:T(8,128)S(1)} %get-tuple-element.25), channel_id=1, source_target_pairs={{0,16},{1,17},{2,18},{3,19},{4,20},{5,21},{6,22},{7,23},{8,24},{9,... | collective-permute-start | bytes 614408 | tf_op jit(solution)/shard_map/ppermute | solution.py:292
  36.7 11.9 %collective-permute-start.7 = (f32[200,256]{1,0:T(8,128)S(1)}, f32[200,256]{1,0:T(8,128)S(1)}, u32[]{:S(2)}, u32[]{:S(2)}) collective-permute-start(f32[200,256]{1,0:T(8,128)S(1)} %get-tuple-element.25), channel_id=1, source_target_pairs={{0,8},{1,9},{2,10},{3,11},{4,12},{5,13},{6,14},{7,15},{8,16},{9,17... | collective-permute-start | bytes 614408 | tf_op jit(solution)/shard_map/ppermute | solution.py:292
  44.9 3.7 %collective-permute-start.12 = (f32[200,256]{1,0:T(8,128)S(1)}, f32[200,256]{1,0:T(8,128)S(1)}, u32[]{:S(2)}, u32[]{:S(2)}) collective-permute-start(f32[200,256]{1,0:T(8,128)S(1)} %collective-permute-done.9.refs_4_), channel_id=1, source_target_pairs={{0,1},{1,0},{2,3},{3,2},{4,5},{5,4},{6,7},{7,6},{8,9},{9,8},{10,11... | collective-permute-start | bytes 614408 | tf_op jit(solution)/shard_map/ppermute | solution.py:292
  45.4 3.2 %collective-permute-start.11 = (f32[200,256]{1,0:T(8,128)S(1)}, f32[200,256]{1,0:T(8,128)S(1)}, u32[]{:S(2)}, u32[]{:S(2)}) collective-permute-start(f32[200,256]{1,0:T(8,128)S(1)} %collective-permute-done.8.refs_3_), channel_id=1, source_target_pairs={{0,1},{1,0},{2,3},{3,2},{4,5},{5,4},{6,7},{7,6},{8,9},{9,8},{10,11... | collective-permute-start | bytes 614408 | tf_op jit(solution)/shard_map/ppermute | solution.py:292
  48.6 1.5 collective-permute-start.10
  53.7 13.1 %collective-permute-start.15 = (f32[200,256]{1,0:T(8,128)S(1)}, f32[200,256]{1,0:T(8,128)S(1)}, u32[]{:S(2)}, u32[]{:S(2)}) collective-permute-start(f32[200,256]{1,0:T(8,128)S(1)} %get-tuple-element.26), channel_id=1, source_target_pairs={{0,96},{1,97},{2,98},{3,99},{4,100},{5,101},{6,102},{7,103},{8,104... | collective-permute-start | bytes 614408 | tf_op jit(solution)/shard_map/ppermute | solution.py:292
  57.8 9.5 %collective-permute-start.14 = (f32[200,256]{1,0:T(8,128)S(1)}, f32[200,256]{1,0:T(8,128)S(1)}, u32[]{:S(2)}, u32[]{:S(2)}) collective-permute-start(f32[200,256]{1,0:T(8,128)S(1)} %get-tuple-element.26), channel_id=1, source_target_pairs={{0,64},{1,65},{2,66},{3,67},{4,68},{5,69},{6,70},{7,71},{8,72},{9,... | collective-permute-start | bytes 614408 | tf_op jit(solution)/shard_map/ppermute | solution.py:292
  57.8 12.4 %collective-permute-start.13 = (f32[200,256]{1,0:T(8,128)S(1)}, f32[200,256]{1,0:T(8,128)S(1)}, u32[]{:S(2)}, u32[]{:S(2)}) collective-permute-start(f32[200,256]{1,0:T(8,128)S(1)} %get-tuple-element.26), channel_id=1, source_target_pairs={{0,32},{1,33},{2,34},{3,35},{4,36},{5,37},{6,38},{7,39},{8,40},{9,... | collective-permute-start | bytes 614408 | tf_op jit(solution)/shard_map/ppermute | solution.py:292
  66.8 3.4 %collective-permute-start.18 = (f32[200,256]{1,0:T(8,128)S(1)}, f32[200,256]{1,0:T(8,128)S(1)}, u32[]{:S(2)}, u32[]{:S(2)}) collective-permute-start(f32[200,256]{1,0:T(8,128)S(1)} %collective-permute-done.15.r3), channel_id=1, source_target_pairs={{0,1},{1,0},{2,3},{3,2},{4,5},{5,4},{6,7},{7,6},{8,9},{9,8},{10,11... | collective-permute-start | bytes 614408 | tf_op jit(solution)/shard_map/ppermute | solution.py:292
  67.2 3.0 %collective-permute-start.17 = (f32[200,256]{1,0:T(8,128)S(1)}, f32[200,256]{1,0:T(8,128)S(1)}, u32[]{:S(2)}, u32[]{:S(2)}) collective-permute-start(f32[200,256]{1,0:T(8,128)S(1)} %collective-permute-done.14.r2), channel_id=1, source_target_pairs={{0,1},{1,0},{2,3},{3,2},{4,5},{5,4},{6,7},{7,6},{8,9},{9,8},{10,11... | collective-permute-start | bytes 614408 | tf_op jit(solution)/shard_map/ppermute | solution.py:292
  70.2 1.5 collective-permute-start.16
  160.8 1.7 collective-permute-start.19
  162.5 3.6 %collective-permute-start.22 = (f32[8,128]{1,0:T(8,128)S(1)}, f32[8,128]{1,0:T(8,128)S(1)}, u32[]{:S(2)}, u32[]{:S(2)}) collective-permute-start(f32[8,128]{1,0:T(8,128)S(1)} %add.30), channel_id=1, source_target_pairs={{0,6},{1,7},{2,0},{3,1},{4,2},{5,3},{6,4},{7,5},{8,14},{9,15},{10,... | collective-permute-start | bytes 12296 | tf_op jit(solution)/shard_map/ppermute | solution.py:292
  163.2 4.8 %collective-permute-start.21 = (f32[8,128]{1,0:T(8,128)S(1)}, f32[8,128]{1,0:T(8,128)S(1)}, u32[]{:S(2)}, u32[]{:S(2)}) collective-permute-start(f32[8,128]{1,0:T(8,128)S(1)} %add.30), channel_id=1, source_target_pairs={{0,2},{1,3},{2,4},{3,5},{4,6},{5,7},{6,0},{7,1},{8,10},{9,11},{10,... | collective-permute-start | bytes 12296 | tf_op jit(solution)/shard_map/ppermute | solution.py:292
  164.5 5.1 %collective-permute-start.20 = (f32[8,128]{1,0:T(8,128)S(1)}, f32[8,128]{1,0:T(8,128)S(1)}, u32[]{:S(2)}, u32[]{:S(2)}) collective-permute-start(f32[8,128]{1,0:T(8,128)S(1)} %add.30), channel_id=1, source_target_pairs={{0,4},{1,5},{2,6},{3,7},{4,0},{5,1},{6,2},{7,3},{8,12},{9,13},{10,... | collective-permute-start | bytes 12296 | tf_op jit(solution)/shard_map/ppermute | solution.py:292
  169.6 3.6 %collective-permute-start.25 = (f32[8,128]{1,0:T(8,128)S(1)}, f32[8,128]{1,0:T(8,128)S(1)}, u32[]{:S(2)}, u32[]{:S(2)}) collective-permute-start(f32[8,128]{1,0:T(8,128)S(1)} %add_add_fusion.2), channel_id=1, source_target_pairs={{0,24},{1,25},{2,26},{3,27},{4,28},{5,29},{6,30},{7,31},{8,0},{9,1... | collective-permute-start | bytes 12296 | tf_op jit(solution)/shard_map/ppermute | solution.py:292
  170.3 4.8 %collective-permute-start.24 = (f32[8,128]{1,0:T(8,128)S(1)}, f32[8,128]{1,0:T(8,128)S(1)}, u32[]{:S(2)}, u32[]{:S(2)}) collective-permute-start(f32[8,128]{1,0:T(8,128)S(1)} %add_add_fusion.2), channel_id=1, source_target_pairs={{0,8},{1,9},{2,10},{3,11},{4,12},{5,13},{6,14},{7,15},{8,16},{9,17... | collective-permute-start | bytes 12296 | tf_op jit(solution)/shard_map/ppermute | solution.py:292
  171.7 5.1 %collective-permute-start.23 = (f32[8,128]{1,0:T(8,128)S(1)}, f32[8,128]{1,0:T(8,128)S(1)}, u32[]{:S(2)}, u32[]{:S(2)}) collective-permute-start(f32[8,128]{1,0:T(8,128)S(1)} %add_add_fusion.2), channel_id=1, source_target_pairs={{0,16},{1,17},{2,18},{3,19},{4,20},{5,21},{6,22},{7,23},{8,24},{9,... | collective-permute-start | bytes 12296 | tf_op jit(solution)/shard_map/ppermute | solution.py:292
  176.8 4.5 %collective-permute-start.28 = (f32[8,128]{1,0:T(8,128)S(1)}, f32[8,128]{1,0:T(8,128)S(1)}, u32[]{:S(2)}, u32[]{:S(2)}) collective-permute-start(f32[8,128]{1,0:T(8,128)S(1)} %add_add_fusion.1), channel_id=1, source_target_pairs={{0,96},{1,97},{2,98},{3,99},{4,100},{5,101},{6,102},{7,103},{8,104... | collective-permute-start | bytes 12296 | tf_op jit(solution)/shard_map/ppermute | solution.py:292
  179.8 4.8 %collective-permute-start.27 = (f32[8,128]{1,0:T(8,128)S(1)}, f32[8,128]{1,0:T(8,128)S(1)}, u32[]{:S(2)}, u32[]{:S(2)}) collective-permute-start(f32[8,128]{1,0:T(8,128)S(1)} %add_add_fusion.1), channel_id=1, source_target_pairs={{0,32},{1,33},{2,34},{3,35},{4,36},{5,37},{6,38},{7,39},{8,40},{9,... | collective-permute-start | bytes 12296 | tf_op jit(solution)/shard_map/ppermute | solution.py:292
  179.8 5.1 %collective-permute-start.26 = (f32[8,128]{1,0:T(8,128)S(1)}, f32[8,128]{1,0:T(8,128)S(1)}, u32[]{:S(2)}, u32[]{:S(2)}) collective-permute-start(f32[8,128]{1,0:T(8,128)S(1)} %add_add_fusion.1), channel_id=1, source_target_pairs={{0,64},{1,65},{2,66},{3,67},{4,68},{5,69},{6,70},{7,71},{8,72},{9,... | collective-permute-start | bytes 12296 | tf_op jit(solution)/shard_map/ppermute | solution.py:292

commit v2 on v1

--- a/solution.py
+++ b/solution.py
@@ -13,6 +13,7 @@
 ROWS = 400
 HALF = ROWS // 2
 PB = 8
+NB = 32
 
 
 def split(x):
@@ -156,76 +157,69 @@
 
 
 def lane(x, i):
-    return jnp.take_along_axis(
-        x, jnp.full(x.shape, i, jnp.int32), axis=1, mode="promise_in_bounds"
-    )
-
-
-def factor(rows, n):
-    width = len(rows)
-
-    def panel(q, _):
-        j0 = q * PB
-        held = [[ref[pl.ds((j0 + t) * 8, 8), :] for t in range(PB)] for ref in rows]
+    return jnp.broadcast_to(x[:, i : i + 1], x.shape)
+
+
+def factor_block(rows, o):
+    tiles, count = len(rows), len(rows[0])
+    for q in range(0, count, PB):
+        a = {(t, s): lane(rows[0][q + t], o + q + s) for t in range(PB) for s in range(t, PB)}
         for t in range(PB):
-            inv = lax.rsqrt(lane(held[0][t], j0 + t))
-            for w in range(width):
-                held[w][t] = held[w][t] * inv
+            inv = lax.rsqrt(a[t, t])
+            u = {s: a[t, s] * inv for s in range(t + 1, PB)}
             for s in range(t + 1, PB):
-                c = lane(held[0][t], j0 + s)
-                for w in range(width):
-                    held[w][s] = held[w][s] - c * held[w][t]
-        for w in range(width):
+                for r in range(s, PB):
+                    a[s, r] = a[s, r] - u[s] * u[r]
+            for w in range(tiles):
+                rows[w][q + t] = rows[w][q + t] * inv
+                for s in range(t + 1, PB):
+                    rows[w][q + s] = rows[w][q + s] - u[s] * rows[w][q + t]
+        for i in range(q + PB, count):
             for t in range(PB):
-                rows[w][pl.ds((j0 + t) * 8, 8), :] = held[w][t]
-
-        def trail(p, _):
-            i0 = p * PB
-            for s in range(PB):
-                acc = [rows[w][pl.ds((i0 + s) * 8, 8), :] for w in range(width)]
-                for t in range(PB):
-                    c = lane(held[0][t], i0 + s)
-                    for w in range(width):
-                        acc[w] = acc[w] - c * held[w][t]
-                for w in range(width):
-                    rows[w][pl.ds((i0 + s) * 8, 8), :] = acc[w]
-            return 0
-
-        lax.fori_loop(q + 1, n // PB, trail, 0)
-        return 0
-
-    lax.fori_loop(0, n // PB, panel, 0)
-
-
-def strided(m):
-    return pl.ds(m, H, stride=STEPS)
-
-
-def cholesky(cov, l_ref, logs_ref, d1, b1, d2):
-    for m in range(STEPS):
-        d1[strided(m), :] = cov[m, 0:H, 0:H]
-        b1[strided(m), :] = cov[m, 0:H, H:]
-    factor([d1, b1], H)
-    for m in range(STEPS):
-        u = split(b1[strided(m), :])
-        d2[strided(m), :] = cov[m, H:, H:] - mm3(u, u, 0, 0)
-    factor([d2], H)
+                c = lane(rows[0][q + t], o + i)
+                for w in range(tiles):
+                    rows[w][i] = rows[w][i] - c * rows[w][q + t]
+
+
+def strided(j, count, m):
+    return pl.ds(STEPS * j + m, count, stride=STEPS)
+
+
+def cholesky(cov, l_ref, logs_ref, u0, u1):
+    us = (u0, u1)
+    for j0 in range(0, N, NB):
+        first, r0 = j0 // H, j0 + NB
+        tiles = range(first, 2)
+        for m in range(STEPS):
+            for w in tiles:
+                us[w][strided(j0, NB, m), :] = cov[m, j0:r0, H * w : H * w + H]
+        rows = [[us[w][pl.ds(8 * (j0 + i), 8), :] for i in range(NB)] for w in tiles]
+        factor_block(rows, j0 % H)
+        for w in tiles:
+            for i in range(NB):
+                us[w][pl.ds(8 * (j0 + i), 8), :] = rows[w - first][i]
+        if r0 == N:
+            break
+        for m in range(STEPS):
+            u = jnp.concatenate([us[w][strided(j0, NB, m), :] for w in tiles], axis=1)
+            left, right = split(u.T[r0 - H * first :, :]), split(u)
+            cov[m, r0:, H * first :] = cov[m, r0:, H * first :] - mm3(left, right)
     r, c = grid_iota()
     total = jnp.zeros((1, H), f32)
     for m in range(STEPS):
-        u1 = d1[strided(m), :]
-        u2 = d2[strided(m), :]
-        logs = jnp.log(jnp.where(r == c, u1, 1.0)) + jnp.log(jnp.where(r == c, u2, 1.0))
+        a1 = u0[strided(0, H, m), :]
+        a2 = u1[strided(H, H, m), :]
+        logs = jnp.log(jnp.where(r == c, a1, 1.0)) + jnp.log(jnp.where(r == c, a2, 1.0))
         total = total + jnp.sum(logs, axis=0, keepdims=True)
-        l_ref[m, 0:H, 0:H] = jnp.where(r <= c, u1, 0.0).T
-        l_ref[m, H:, 0:H] = b1[strided(m), :].T
-        l_ref[m, H:, H:] = jnp.where(r <= c, u2, 0.0).T
+        l_ref[m, 0:H, 0:H] = jnp.where(r <= c, a1, 0.0).T
+        l_ref[m, H:, 0:H] = u1[strided(0, H, m), :].T
+        l_ref[m, H:, H:] = jnp.where(r <= c, a2, 0.0).T
         l_ref[m, 0:H, H:] = jnp.zeros((H, H), f32)
     logs_ref[...] = jnp.broadcast_to(total, (8, H))
 
 
 def final_kernel(place, r1, r2, r3, s1, s2, s3, xa, xz, xb, ya, yz, yb, core, a_ref, p_ref, b_ref, m0_ref, l0_ref,
-                 means, l_ref, logs, pieces, zs, ms, cov, d1, b1, d2):
+                 means, l_ref, logs, pieces, zs, ms, cov, u0, u1):
     me, c = place[0], place[3]
     here = pl.multiple_of(c * HALF, 8)
     there = pl.multiple_of((1 - c) * HALF, 8)
@@ -256,7 +250,7 @@
         a = split(a_ref[k])
         cov[k] = mm3(split(mm3(a, state)), a, 1, 1) + p_ref[k]
         means[k : k + 1, :] = (row_times(mean, a) + b_ref[k])[0:1, :]
-    cholesky(cov, l_ref, logs, d1, b1, d2)
+    cholesky(cov, l_ref, logs, u0, u1)
 
 
 VMEM = pl.BlockSpec(memory_space=pltpu.VMEM)
@@ -327,9 +321,8 @@
             pltpu.VMEM((N, N), f32),
             pltpu.VMEM((8, N), f32),
             pltpu.VMEM((STEPS, N, N), f32),
-            pltpu.VMEM((STEPS * H, H), f32),
-            pltpu.VMEM((STEPS * H, H), f32),
-            pltpu.VMEM((STEPS * H, H), f32),
+            pltpu.VMEM((STEPS * N, H), f32),
+            pltpu.VMEM((STEPS * N, H), f32),
         ],
         "final",
     )(place, *gather_ring(mine, "z"), *by_x, *by_y, other, a, p, b, initial_mean[None], initial_factor)

time: 188 us -> 121 us (0.64)
  Pallas kernels: 104 us -> 37.6 us
    pallas_call x1, Pallas kernels: 89.2 us -> 22.7 us  [on_device(): call(final_kernel, (shape(STEPS, N), stack, shape(8, H)), [SMEM] + [VMEM]...]
where the time goes in v2:
time: 121 us
  waiting for transfers between devices  52.3 us (43%)
  Pallas kernels  37.6 us (31%)
  starting transfers between devices  25.7 us (21%)
  between operations  2.49 us (2%)
  local copies, waits for them, and re-layouts  2.04 us (2%)
    ppermute x29, waiting for transfers between devices, send(): return lax.ppermute(x, AXES, ring(axis, back))  52.3 us
    ppermute x29, starting transfers between devices, send(): return lax.ppermute(x, AXES, ring(axis, back))  25.7 us
    pallas_call x1, Pallas kernels, on_device(): call(final_kernel, (shape(STEPS, N), stack, shape(8, H)), [SMEM] + [VMEM]...  22.7 us
    pallas_call x1, Pallas kernels, on_device(): call(local_kernel, (stack, stack, shape(STEPS, 8, N), packed), [VMEM] * 3...  7.16 us
    pallas_call x2, Pallas kernels, on_device(): call(lambda *refs, which=which: ring_kernel(which, *refs), (half, packed)...  6.45 us
  transfers between devices with their start and end apart: 29, of which 22 were waited for; matrix products, arithmetic and copies ran while one was open for 0% of the time, Pallas kernels for 0%

profile of v2, /device:TPU:0, one launch (start us, length us, event | category | flops | bytes accessed | tf_op | source)
XLA Modules:
  0.0 120.9 jit_solution(12896042012270545834)
XLA Ops:
  0.6 0.7 copy-done.2
  1.3 7.2 %local.1 = (f32[8,256,256]{2,1,0:T(8,128)S(1)}, f32[8,256,256]{2,1,0:T(8,128)S(1)}, f32[8,8,256]{2,1,0:T(8,128)S(1)}, f32[400,256]{1,0:T(8,128)S(1)}) custom-call(f32[8,256,256]{2,1,0:T(8,128)} %t_ref.1, f32[8,256,256]{2,1,0:T(8,128)} %n_ref.1, f32[8,256]{1,0:T(8,128)S(1)} %copy-done.2), custom_call_target="tpu_custom_call" | custom-call | tf_op jit(solution)/shard_map/local/pallas_call | solution.py:299
  8.5 1.3 %copy-done = f32[8,256,256]{2,1,0:T(8,128)} copy-done((f32[8,256,256]{2,1,0:T(8,128)}, f32[8,256,256]{2,1,0:T(8,128)S(1)}, u32[]{:S(2)}) %copy-start) | copy-done | bytes 2097176
  9.8 0.0 collective-permute-start
  9.8 0.1 pad_add_fusion.place.refs_0_
  9.9 1.7 %collective-permute-done.other.core = f32[400,256]{1,0:T(8,128)S(1)} collective-permute-done((f32[400,256]{1,0:T(8,128)S(1)}, f32[400,256]{1,0:T(8,128)S(1)}, u32[]{:S(2)}, u32[]{:S(2)}) %collective-permute-start) | collective-permute-done | bytes 409632 | tf_op jit(solution)/shard_map/ppermute | solution.py:286
  11.6 1.3 %core.1 = (f32[200,256]{1,0:T(8,128)S(1)}, f32[400,256]{1,0:T(8,128)S(1)}) custom-call(s32[4]{0:T(128)S(1)} %pad_add_fusion.place.refs_0_, f32[400,256]{1,0:T(8,128)S(1)} %get-tuple-element.21.own, f32[400,256]{1,0:T(8,128)S(1)} %collective-permute-done.other.core), custom_call_target="tpu_custom_call" | custom-call | tf_op jit(solution)/shard_map/core/pallas_call | solution.py:303
  12.9 3.2 %collective-permute-start.3 = (f32[200,256]{1,0:T(8,128)S(1)}, f32[200,256]{1,0:T(8,128)S(1)}, u32[]{:S(2)}, u32[]{:S(2)}) collective-permute-start(f32[200,256]{1,0:T(8,128)S(1)} %get-tuple-element.23), channel_id=1, source_target_pairs={{0,6},{1,7},{2,0},{3,1},{4,2},{5,3},{6,4},{7,5},{8,14},{9,15},{10,... | collective-permute-start | bytes 614408 | tf_op jit(solution)/shard_map/ppermute | solution.py:286
  16.1 0.6 collective-permute-start.2
  16.7 1.0 collective-permute-start.1
  17.7 7.4 %collective-permute-done.3.refs_4_ = f32[200,256]{1,0:T(8,128)S(1)} collective-permute-done((f32[200,256]{1,0:T(8,128)S(1)}, f32[200,256]{1,0:T(8,128)S(1)}, u32[]{:S(2)}, u32[]{:S(2)}) %collective-permute-start.3) | collective-permute-done | bytes 204832 | tf_op jit(solution)/shard_map/ppermute | solution.py:286
  25.1 0.0 collective-permute-start.6
  25.1 0.5 collective-permute-done.2.refs_3_
  25.6 0.0 collective-permute-start.5
  25.6 3.2 %collective-permute-done.1.refs_2_ = f32[200,256]{1,0:T(8,128)S(1)} collective-permute-done((f32[200,256]{1,0:T(8,128)S(1)}, f32[200,256]{1,0:T(8,128)S(1)}, u32[]{:S(2)}, u32[]{:S(2)}) %collective-permute-start.1) | collective-permute-done | bytes 204832 | tf_op jit(solution)/shard_map/ppermute | solution.py:286
  28.8 0.0 collective-permute-start.4
  28.8 0.0 collective-permute-done.6.refs_7_
  28.8 1.4 %collective-permute-done.4.refs_5_ = f32[200,256]{1,0:T(8,128)S(1)} collective-permute-done((f32[200,256]{1,0:T(8,128)S(1)}, f32[200,256]{1,0:T(8,128)S(1)}, u32[]{:S(2)}, u32[]{:S(2)}) %collective-permute-start.4) | collective-permute-done | bytes 204832 | tf_op jit(solution)/shard_map/ppermute | solution.py:286
  30.3 2.8 %ring_y.1 = (f32[200,256]{1,0:T(8,128)S(1)}, f32[400,256]{1,0:T(8,128)S(1)}, f32[256,256]{1,0:T(8,128)S(1)}, f32[256,256]{1,0:T(8,128)S(1)}, f32[8,256]{1,0:T(8,128)S(1)}) custom-call(s32[4]{0:T(128)S(1)} %pad_add_fusion.place.refs_0_, f32[400,256]{1,0:T(8,128)S(1)} %get-tuple-element.22.refs_1_, f32[200,256]{1,0:T(8,128)S(1)} %collective-permute-done.1.refs_2_, ...), custom_call_target="tpu_custom_call" | custom-call | tf_op jit(solution)/shard_map/ring_y/pallas_call | solution.py:306
  33.0 2.8 %collective-permute-start.9 = (f32[200,256]{1,0:T(8,128)S(1)}, f32[200,256]{1,0:T(8,128)S(1)}, u32[]{:S(2)}, u32[]{:S(2)}) collective-permute-start(f32[200,256]{1,0:T(8,128)S(1)} %get-tuple-element.25), channel_id=1, source_target_pairs={{0,24},{1,25},{2,26},{3,27},{4,28},{5,29},{6,30},{7,31},{8,0},{9,1... | collective-permute-start | bytes 614408 | tf_op jit(solution)/shard_map/ppermute | solution.py:286
  35.9 0.8 collective-permute-start.8
  36.7 0.9 collective-permute-start.7
  37.5 7.4 %collective-permute-done.9.refs_4_ = f32[200,256]{1,0:T(8,128)S(1)} collective-permute-done((f32[200,256]{1,0:T(8,128)S(1)}, f32[200,256]{1,0:T(8,128)S(1)}, u32[]{:S(2)}, u32[]{:S(2)}) %collective-permute-start.9) | collective-permute-done | bytes 204832 | tf_op jit(solution)/shard_map/ppermute | solution.py:286
  44.9 0.0 collective-permute-start.12
  44.9 0.4 collective-permute-done.8.refs_3_
  45.4 0.1 collective-permute-start.11
  45.4 3.2 %collective-permute-done.7.refs_2_ = f32[200,256]{1,0:T(8,128)S(1)} collective-permute-done((f32[200,256]{1,0:T(8,128)S(1)}, f32[200,256]{1,0:T(8,128)S(1)}, u32[]{:S(2)}, u32[]{:S(2)}) %collective-permute-start.7) | collective-permute-done | bytes 204832 | tf_op jit(solution)/shard_map/ppermute | solution.py:286
  48.6 0.0 collective-permute-start.10
  48.6 0.0 collective-permute-done.12.refs_7_
  48.6 1.4 %collective-permute-done.10.refs_5_ = f32[200,256]{1,0:T(8,128)S(1)} collective-permute-done((f32[200,256]{1,0:T(8,128)S(1)}, f32[200,256]{1,0:T(8,128)S(1)}, u32[]{:S(2)}, u32[]{:S(2)}) %collective-permute-start.10) | collective-permute-done | bytes 204832 | tf_op jit(solution)/shard_map/ppermute | solution.py:286
  50.0 3.7 %ring_x.1 = (f32[200,256]{1,0:T(8,128)S(1)}, f32[400,256]{1,0:T(8,128)}, f32[256,256]{1,0:T(8,128)S(1)}, f32[256,256]{1,0:T(8,128)S(1)}, f32[8,256]{1,0:T(8,128)S(1)}) custom-call(s32[4]{0:T(128)S(1)} %pad_add_fusion.place.refs_0_, f32[400,256]{1,0:T(8,128)S(1)} %get-tuple-element.24.refs_1_, f32[200,256]{1,0:T(8,128)S(1)} %collective-permute-done.7.refs_2_, ...), custom_call_target="tpu_custom_call" | custom-call | tf_op jit(solution)/shard_map/ring_x/pallas_call | solution.py:306
  53.7 4.0 %collective-permute-start.15 = (f32[200,256]{1,0:T(8,128)S(1)}, f32[200,256]{1,0:T(8,128)S(1)}, u32[]{:S(2)}, u32[]{:S(2)}) collective-permute-start(f32[200,256]{1,0:T(8,128)S(1)} %get-tuple-element.26), channel_id=1, source_target_pairs={{0,96},{1,97},{2,98},{3,99},{4,100},{5,101},{6,102},{7,103},{8,104... | collective-permute-start | bytes 614408 | tf_op jit(solution)/shard_map/ppermute | solution.py:286
  57.8 0.0 collective-permute-start.14
  57.8 1.3 %collective-permute-start.13 = (f32[200,256]{1,0:T(8,128)S(1)}, f32[200,256]{1,0:T(8,128)S(1)}, u32[]{:S(2)}, u32[]{:S(2)}) collective-permute-start(f32[200,256]{1,0:T(8,128)S(1)} %get-tuple-element.26), channel_id=1, source_target_pairs={{0,32},{1,33},{2,34},{3,35},{4,36},{5,37},{6,38},{7,39},{8,40},{9,... | collective-permute-start | bytes 614408 | tf_op jit(solution)/shard_map/ppermute | solution.py:286
  59.0 7.8 %collective-permute-done.15.r3 = f32[200,256]{1,0:T(8,128)S(1)} collective-permute-done((f32[200,256]{1,0:T(8,128)S(1)}, f32[200,256]{1,0:T(8,128)S(1)}, u32[]{:S(2)}, u32[]{:S(2)}) %collective-permute-start.15) | collective-permute-done | bytes 204832 | tf_op jit(solution)/shard_map/ppermute | solution.py:286
  66.8 0.0 collective-permute-start.18
  66.8 0.4 collective-permute-done.14.r2
  67.2 0.1 collective-permute-start.17
  67.3 2.9 %collective-permute-done.13.r1 = f32[200,256]{1,0:T(8,128)S(1)} collective-permute-done((f32[200,256]{1,0:T(8,128)S(1)}, f32[200,256]{1,0:T(8,128)S(1)}, u32[]{:S(2)}, u32[]{:S(2)}) %collective-permute-start.13) | collective-permute-done | bytes 204832 | tf_op jit(solution)/shard_map/ppermute | solution.py:286
  70.2 0.0 collective-permute-start.16
  70.2 0.0 collective-permute-done.18.s3
  70.2 0.0 collective-permute-done.17.s2
  70.2 1.4 %collective-permute-done.16.s1 = f32[200,256]{1,0:T(8,128)S(1)} collective-permute-done((f32[200,256]{1,0:T(8,128)S(1)}, f32[200,256]{1,0:T(8,128)S(1)}, u32[]{:S(2)}, u32[]{:S(2)}) %collective-permute-start.16) | collective-permute-done | bytes 204832 | tf_op jit(solution)/shard_map/ppermute | solution.py:286
  71.7 22.7 %final.1 = (f32[8,256]{1,0:T(8,128)}, f32[8,256,256]{2,1,0:T(8,128)}, f32[8,128]{1,0:T(8,128)S(1)}) custom-call(s32[4]{0:T(128)S(1)} %pad_add_fusion.place.refs_0_, f32[200,256]{1,0:T(8,128)S(1)} %collective-permute-done.13.r1, f32[200,256]{1,0:T(8,128)S(1)} %collective-permute-done.14.r2, f32[200,256]{1,0:T(8,128)S(1)} %collective-permute-done.15.r3, ...), custom_call_target="tpu_custom_call" | custom-call | tf_op jit(solution)/shard_map/final/pallas_call | solution.py:315
  94.4 0.8 collective-permute-start.19
  95.2 0.8 collective-permute-done.19
  96.1 0.7 collective-permute-start.22
  96.8 1.3 %collective-permute-start.21 = (f32[8,128]{1,0:T(8,128)S(1)}, f32[8,128]{1,0:T(8,128)S(1)}, u32[]{:S(2)}, u32[]{:S(2)}) collective-permute-start(f32[8,128]{1,0:T(8,128)S(1)} %add.30), channel_id=1, source_target_pairs={{0,2},{1,3},{2,4},{3,5},{4,6},{5,7},{6,0},{7,1},{8,10},{9,11},{10,... | collective-permute-start | bytes 12296 | tf_op jit(solution)/shard_map/ppermute | solution.py:286
  98.1 0.7 collective-permute-start.20
  98.8 0.9 collective-permute-done.22
  99.7 1.9 %collective-permute-done.21 = f32[8,128]{1,0:T(8,128)S(1)} collective-permute-done((f32[8,128]{1,0:T(8,128)S(1)}, f32[8,128]{1,0:T(8,128)S(1)}, u32[]{:S(2)}, u32[]{:S(2)}) %collective-permute-start.21) | collective-permute-done | bytes 4128 | tf_op jit(solution)/shard_map/ppermute | solution.py:286
  101.6 1.6 %collective-permute-done.20 = f32[8,128]{1,0:T(8,128)S(1)} collective-permute-done((f32[8,128]{1,0:T(8,128)S(1)}, f32[8,128]{1,0:T(8,128)S(1)}, u32[]{:S(2)}, u32[]{:S(2)}) %collective-permute-start.20) | collective-permute-done | bytes 4128 | tf_op jit(solution)/shard_map/ppermute | solution.py:286
  103.2 0.7 collective-permute-start.25
  103.9 1.3 %collective-permute-start.24 = (f32[8,128]{1,0:T(8,128)S(1)}, f32[8,128]{1,0:T(8,128)S(1)}, u32[]{:S(2)}, u32[]{:S(2)}) collective-permute-start(f32[8,128]{1,0:T(8,128)S(1)} %add_add_fusion.2), channel_id=1, source_target_pairs={{0,8},{1,9},{2,10},{3,11},{4,12},{5,13},{6,14},{7,15},{8,16},{9,17... | collective-permute-start | bytes 12296 | tf_op jit(solution)/shard_map/ppermute | solution.py:286
  105.2 0.8 collective-permute-start.23
  106.1 0.8 collective-permute-done.25
  106.8 1.9 %collective-permute-done.24 = f32[8,128]{1,0:T(8,128)S(1)} collective-permute-done((f32[8,128]{1,0:T(8,128)S(1)}, f32[8,128]{1,0:T(8,128)S(1)}, u32[]{:S(2)}, u32[]{:S(2)}) %collective-permute-start.24) | collective-permute-done | bytes 4128 | tf_op jit(solution)/shard_map/ppermute | solution.py:286
  108.7 1.6 %collective-permute-done.23 = f32[8,128]{1,0:T(8,128)S(1)} collective-permute-done((f32[8,128]{1,0:T(8,128)S(1)}, f32[8,128]{1,0:T(8,128)S(1)}, u32[]{:S(2)}, u32[]{:S(2)}) %collective-permute-start.23) | collective-permute-done | bytes 4128 | tf_op jit(solution)/shard_map/ppermute | solution.py:286
  110.4 3.0 %collective-permute-start.28 = (f32[8,128]{1,0:T(8,128)S(1)}, f32[8,128]{1,0:T(8,128)S(1)}, u32[]{:S(2)}, u32[]{:S(2)}) collective-permute-start(f32[8,128]{1,0:T(8,128)S(1)} %add_add_fusion.1), channel_id=1, source_target_pairs={{0,96},{1,97},{2,98},{3,99},{4,100},{5,101},{6,102},{7,103},{8,104... | collective-permute-start | bytes 12296 | tf_op jit(solution)/shard_map/ppermute | solution.py:286
  113.4 0.0 collective-permute-start.27
  113.4 1.5 %collective-permute-start.26 = (f32[8,128]{1,0:T(8,128)S(1)}, f32[8,128]{1,0:T(8,128)S(1)}, u32[]{:S(2)}, u32[]{:S(2)}) collective-permute-start(f32[8,128]{1,0:T(8,128)S(1)} %add_add_fusion.1), channel_id=1, source_target_pairs={{0,64},{1,65},{2,66},{3,67},{4,68},{5,69},{6,70},{7,71},{8,72},{9,... | collective-permute-start | bytes 12296 | tf_op jit(solution)/shard_map/ppermute | solution.py:286
  114.9 3.3 %collective-permute-done.27 = f32[8,128]{1,0:T(8,128)S(1)} collective-permute-done((f32[8,128]{1,0:T(8,128)S(1)}, f32[8,128]{1,0:T(8,128)S(1)}, u32[]{:S(2)}, u32[]{:S(2)}) %collective-permute-start.27) | collective-permute-done | bytes 4128 | tf_op jit(solution)/shard_map/ppermute | solution.py:286
  118.2 0.3 collective-permute-done.26
  118.5 0.6 slice_reduce_fusion
  (13 shorter events, 0.0 us)
Async XLA Ops:
  0.6 0.7 copy-start.2
  8.5 1.3 %copy-start = (f32[8,256,256]{2,1,0:T(8,128)}, f32[8,256,256]{2,1,0:T(8,128)S(1)}, u32[]{:S(2)}) copy-start(f32[8,256,256]{2,1,0:T(8,128)S(1)} %get-tuple-element.34.p_ref) | copy-start | bytes 6291460
  9.8 61.8 %copy-start.1 = (f32[256,256]{1,0:T(8,128)S(1)}, f32[256,256]{1,0:T(8,128)}, u32[]{:S(2)}) copy-start(f32[256,256]{1,0:T(8,128)} %l0_ref.1) | copy-start | bytes 786436
  9.8 61.8 %copy-start.3 = (f32[256]{0:T(256)S(1)}, f32[256]{0:T(256)}, u32[]{:S(2)}) copy-start(f32[256]{0:T(256)} %param.8) | copy-start | bytes 3076
  9.8 1.7 %collective-permute-start = (f32[400,256]{1,0:T(8,128)S(1)}, f32[400,256]{1,0:T(8,128)S(1)}, u32[]{:S(2)}, u32[]{:S(2)}) collective-permute-start(f32[400,256]{1,0:T(8,128)S(1)} %get-tuple-element.21.own), channel_id=1, source_target_pairs={{0,1},{1,0},{2,3},{3,2},{4,5},{5,4},{6,7},{7,6},{8,9},{9,8},{10,11... | collective-permute-start | bytes 1228808 | tf_op jit(solution)/shard_map/ppermute | solution.py:286
  12.9 12.2 %collective-permute-start.3 = (f32[200,256]{1,0:T(8,128)S(1)}, f32[200,256]{1,0:T(8,128)S(1)}, u32[]{:S(2)}, u32[]{:S(2)}) collective-permute-start(f32[200,256]{1,0:T(8,128)S(1)} %get-tuple-element.23), channel_id=1, source_target_pairs={{0,6},{1,7},{2,0},{3,1},{4,2},{5,3},{6,4},{7,5},{8,14},{9,15},{10,... | collective-permute-start | bytes 614408 | tf_op jit(solution)/shard_map/ppermute | solution.py:286
  16.1 9.5 %collective-permute-start.2 = (f32[200,256]{1,0:T(8,128)S(1)}, f32[200,256]{1,0:T(8,128)S(1)}, u32[]{:S(2)}, u32[]{:S(2)}) collective-permute-start(f32[200,256]{1,0:T(8,128)S(1)} %get-tuple-element.23), channel_id=1, source_target_pairs={{0,4},{1,5},{2,6},{3,7},{4,0},{5,1},{6,2},{7,3},{8,12},{9,13},{10,... | collective-permute-start | bytes 614408 | tf_op jit(solution)/shard_map/ppermute | solution.py:286
  16.7 12.1 %collective-permute-start.1 = (f32[200,256]{1,0:T(8,128)S(1)}, f32[200,256]{1,0:T(8,128)S(1)}, u32[]{:S(2)}, u32[]{:S(2)}) collective-permute-start(f32[200,256]{1,0:T(8,128)S(1)} %get-tuple-element.23), channel_id=1, source_target_pairs={{0,2},{1,3},{2,4},{3,5},{4,6},{5,7},{6,0},{7,1},{8,10},{9,11},{10,... | collective-permute-start | bytes 614408 | tf_op jit(solution)/shard_map/ppermute | solution.py:286
  25.1 3.7 %collective-permute-start.6 = (f32[200,256]{1,0:T(8,128)S(1)}, f32[200,256]{1,0:T(8,128)S(1)}, u32[]{:S(2)}, u32[]{:S(2)}) collective-permute-start(f32[200,256]{1,0:T(8,128)S(1)} %collective-permute-done.3.refs_4_), channel_id=1, source_target_pairs={{0,1},{1,0},{2,3},{3,2},{4,5},{5,4},{6,7},{7,6},{8,9},{9,8},{10,11... | collective-permute-start | bytes 614408 | tf_op jit(solution)/shard_map/ppermute | solution.py:286
  25.6 3.2 %collective-permute-start.5 = (f32[200,256]{1,0:T(8,128)S(1)}, f32[200,256]{1,0:T(8,128)S(1)}, u32[]{:S(2)}, u32[]{:S(2)}) collective-permute-start(f32[200,256]{1,0:T(8,128)S(1)} %collective-permute-done.2.refs_3_), channel_id=1, source_target_pairs={{0,1},{1,0},{2,3},{3,2},{4,5},{5,4},{6,7},{7,6},{8,9},{9,8},{10,11... | collective-permute-start | bytes 614408 | tf_op jit(solution)/shard_map/ppermute | solution.py:286
  28.8 1.5 %collective-permute-start.4 = (f32[200,256]{1,0:T(8,128)S(1)}, f32[200,256]{1,0:T(8,128)S(1)}, u32[]{:S(2)}, u32[]{:S(2)}) collective-permute-start(f32[200,256]{1,0:T(8,128)S(1)} %collective-permute-done.1.refs_2_), channel_id=1, source_target_pairs={{0,1},{1,0},{2,3},{3,2},{4,5},{5,4},{6,7},{7,6},{8,9},{9,8},{10,11... | collective-permute-start | bytes 614408 | tf_op jit(solution)/shard_map/ppermute | solution.py:286
  33.0 11.9 %collective-permute-start.9 = (f32[200,256]{1,0:T(8,128)S(1)}, f32[200,256]{1,0:T(8,128)S(1)}, u32[]{:S(2)}, u32[]{:S(2)}) collective-permute-start(f32[200,256]{1,0:T(8,128)S(1)} %get-tuple-element.25), channel_id=1, source_target_pairs={{0,24},{1,25},{2,26},{3,27},{4,28},{5,29},{6,30},{7,31},{8,0},{9,1... | collective-permute-start | bytes 614408 | tf_op jit(solution)/shard_map/ppermute | solution.py:286
  35.9 9.5 %collective-permute-start.8 = (f32[200,256]{1,0:T(8,128)S(1)}, f32[200,256]{1,0:T(8,128)S(1)}, u32[]{:S(2)}, u32[]{:S(2)}) collective-permute-start(f32[200,256]{1,0:T(8,128)S(1)} %get-tuple-element.25), channel_id=1, source_target_pairs={{0,16},{1,17},{2,18},{3,19},{4,20},{5,21},{6,22},{7,23},{8,24},{9,... | collective-permute-start | bytes 614408 | tf_op jit(solution)/shard_map/ppermute | solution.py:286
  36.7 11.9 %collective-permute-start.7 = (f32[200,256]{1,0:T(8,128)S(1)}, f32[200,256]{1,0:T(8,128)S(1)}, u32[]{:S(2)}, u32[]{:S(2)}) collective-permute-start(f32[200,256]{1,0:T(8,128)S(1)} %get-tuple-element.25), channel_id=1, source_target_pairs={{0,8},{1,9},{2,10},{3,11},{4,12},{5,13},{6,14},{7,15},{8,16},{9,17... | collective-permute-start | bytes 614408 | tf_op jit(solution)/shard_map/ppermute | solution.py:286
  44.9 3.7 %collective-permute-start.12 = (f32[200,256]{1,0:T(8,128)S(1)}, f32[200,256]{1,0:T(8,128)S(1)}, u32[]{:S(2)}, u32[]{:S(2)}) collective-permute-start(f32[200,256]{1,0:T(8,128)S(1)} %collective-permute-done.9.refs_4_), channel_id=1, source_target_pairs={{0,1},{1,0},{2,3},{3,2},{4,5},{5,4},{6,7},{7,6},{8,9},{9,8},{10,11... | collective-permute-start | bytes 614408 | tf_op jit(solution)/shard_map/ppermute | solution.py:286
  45.4 3.2 %collective-permute-start.11 = (f32[200,256]{1,0:T(8,128)S(1)}, f32[200,256]{1,0:T(8,128)S(1)}, u32[]{:S(2)}, u32[]{:S(2)}) collective-permute-start(f32[200,256]{1,0:T(8,128)S(1)} %collective-permute-done.8.refs_3_), channel_id=1, source_target_pairs={{0,1},{1,0},{2,3},{3,2},{4,5},{5,4},{6,7},{7,6},{8,9},{9,8},{10,11... | collective-permute-start | bytes 614408 | tf_op jit(solution)/shard_map/ppermute | solution.py:286
  48.6 1.5 %collective-permute-start.10 = (f32[200,256]{1,0:T(8,128)S(1)}, f32[200,256]{1,0:T(8,128)S(1)}, u32[]{:S(2)}, u32[]{:S(2)}) collective-permute-start(f32[200,256]{1,0:T(8,128)S(1)} %collective-permute-done.7.refs_2_), channel_id=1, source_target_pairs={{0,1},{1,0},{2,3},{3,2},{4,5},{5,4},{6,7},{7,6},{8,9},{9,8},{10,11... | collective-permute-start | bytes 614408 | tf_op jit(solution)/shard_map/ppermute | solution.py:286
  53.7 13.1 %collective-permute-start.15 = (f32[200,256]{1,0:T(8,128)S(1)}, f32[200,256]{1,0:T(8,128)S(1)}, u32[]{:S(2)}, u32[]{:S(2)}) collective-permute-start(f32[200,256]{1,0:T(8,128)S(1)} %get-tuple-element.26), channel_id=1, source_target_pairs={{0,96},{1,97},{2,98},{3,99},{4,100},{5,101},{6,102},{7,103},{8,104... | collective-permute-start | bytes 614408 | tf_op jit(solution)/shard_map/ppermute | solution.py:286
  57.8 9.5 %collective-permute-start.14 = (f32[200,256]{1,0:T(8,128)S(1)}, f32[200,256]{1,0:T(8,128)S(1)}, u32[]{:S(2)}, u32[]{:S(2)}) collective-permute-start(f32[200,256]{1,0:T(8,128)S(1)} %get-tuple-element.26), channel_id=1, source_target_pairs={{0,64},{1,65},{2,66},{3,67},{4,68},{5,69},{6,70},{7,71},{8,72},{9,... | collective-permute-start | bytes 614408 | tf_op jit(solution)/shard_map/ppermute | solution.py:286
  57.8 12.4 %collective-permute-start.13 = (f32[200,256]{1,0:T(8,128)S(1)}, f32[200,256]{1,0:T(8,128)S(1)}, u32[]{:S(2)}, u32[]{:S(2)}) collective-permute-start(f32[200,256]{1,0:T(8,128)S(1)} %get-tuple-element.26), channel_id=1, source_target_pairs={{0,32},{1,33},{2,34},{3,35},{4,36},{5,37},{6,38},{7,39},{8,40},{9,... | collective-permute-start | bytes 614408 | tf_op jit(solution)/shard_map/ppermute | solution.py:286
  66.8 3.4 %collective-permute-start.18 = (f32[200,256]{1,0:T(8,128)S(1)}, f32[200,256]{1,0:T(8,128)S(1)}, u32[]{:S(2)}, u32[]{:S(2)}) collective-permute-start(f32[200,256]{1,0:T(8,128)S(1)} %collective-permute-done.15.r3), channel_id=1, source_target_pairs={{0,1},{1,0},{2,3},{3,2},{4,5},{5,4},{6,7},{7,6},{8,9},{9,8},{10,11... | collective-permute-start | bytes 614408 | tf_op jit(solution)/shard_map/ppermute | solution.py:286
  67.2 3.0 %collective-permute-start.17 = (f32[200,256]{1,0:T(8,128)S(1)}, f32[200,256]{1,0:T(8,128)S(1)}, u32[]{:S(2)}, u32[]{:S(2)}) collective-permute-start(f32[200,256]{1,0:T(8,128)S(1)} %collective-permute-done.14.r2), channel_id=1, source_target_pairs={{0,1},{1,0},{2,3},{3,2},{4,5},{5,4},{6,7},{7,6},{8,9},{9,8},{10,11... | collective-permute-start | bytes 614408 | tf_op jit(solution)/shard_map/ppermute | solution.py:286
  70.2 1.5 %collective-permute-start.16 = (f32[200,256]{1,0:T(8,128)S(1)}, f32[200,256]{1,0:T(8,128)S(1)}, u32[]{:S(2)}, u32[]{:S(2)}) collective-permute-start(f32[200,256]{1,0:T(8,128)S(1)} %collective-permute-done.13.r1), channel_id=1, source_target_pairs={{0,1},{1,0},{2,3},{3,2},{4,5},{5,4},{6,7},{7,6},{8,9},{9,8},{10,11... | collective-permute-start | bytes 614408 | tf_op jit(solution)/shard_map/ppermute | solution.py:286
  94.4 1.7 %collective-permute-start.19 = (f32[8,128]{1,0:T(8,128)S(1)}, f32[8,128]{1,0:T(8,128)S(1)}, u32[]{:S(2)}, u32[]{:S(2)}) collective-permute-start(f32[8,128]{1,0:T(8,128)S(1)} %get-tuple-element.38), channel_id=1, source_target_pairs={{0,1},{1,0},{2,3},{3,2},{4,5},{5,4},{6,7},{7,6},{8,9},{9,8},{10,11... | collective-permute-start | bytes 12296 | tf_op jit(solution)/shard_map/ppermute | solution.py:286
  96.1 3.6 %collective-permute-start.22 = (f32[8,128]{1,0:T(8,128)S(1)}, f32[8,128]{1,0:T(8,128)S(1)}, u32[]{:S(2)}, u32[]{:S(2)}) collective-permute-start(f32[8,128]{1,0:T(8,128)S(1)} %add.30), channel_id=1, source_target_pairs={{0,6},{1,7},{2,0},{3,1},{4,2},{5,3},{6,4},{7,5},{8,14},{9,15},{10,... | collective-permute-start | bytes 12296 | tf_op jit(solution)/shard_map/ppermute | solution.py:286
  96.8 4.8 %collective-permute-start.21 = (f32[8,128]{1,0:T(8,128)S(1)}, f32[8,128]{1,0:T(8,128)S(1)}, u32[]{:S(2)}, u32[]{:S(2)}) collective-permute-start(f32[8,128]{1,0:T(8,128)S(1)} %add.30), channel_id=1, source_target_pairs={{0,2},{1,3},{2,4},{3,5},{4,6},{5,7},{6,0},{7,1},{8,10},{9,11},{10,... | collective-permute-start | bytes 12296 | tf_op jit(solution)/shard_map/ppermute | solution.py:286
  98.1 5.1 %collective-permute-start.20 = (f32[8,128]{1,0:T(8,128)S(1)}, f32[8,128]{1,0:T(8,128)S(1)}, u32[]{:S(2)}, u32[]{:S(2)}) collective-permute-start(f32[8,128]{1,0:T(8,128)S(1)} %add.30), channel_id=1, source_target_pairs={{0,4},{1,5},{2,6},{3,7},{4,0},{5,1},{6,2},{7,3},{8,12},{9,13},{10,... | collective-permute-start | bytes 12296 | tf_op jit(solution)/shard_map/ppermute | solution.py:286
  103.2 3.6 %collective-permute-start.25 = (f32[8,128]{1,0:T(8,128)S(1)}, f32[8,128]{1,0:T(8,128)S(1)}, u32[]{:S(2)}, u32[]{:S(2)}) collective-permute-start(f32[8,128]{1,0:T(8,128)S(1)} %add_add_fusion.2), channel_id=1, source_target_pairs={{0,24},{1,25},{2,26},{3,27},{4,28},{5,29},{6,30},{7,31},{8,0},{9,1... | collective-permute-start | bytes 12296 | tf_op jit(solution)/shard_map/ppermute | solution.py:286
  103.9 4.8 %collective-permute-start.24 = (f32[8,128]{1,0:T(8,128)S(1)}, f32[8,128]{1,0:T(8,128)S(1)}, u32[]{:S(2)}, u32[]{:S(2)}) collective-permute-start(f32[8,128]{1,0:T(8,128)S(1)} %add_add_fusion.2), channel_id=1, source_target_pairs={{0,8},{1,9},{2,10},{3,11},{4,12},{5,13},{6,14},{7,15},{8,16},{9,17... | collective-permute-start | bytes 12296 | tf_op jit(solution)/shard_map/ppermute | solution.py:286
  105.2 5.1 %collective-permute-start.23 = (f32[8,128]{1,0:T(8,128)S(1)}, f32[8,128]{1,0:T(8,128)S(1)}, u32[]{:S(2)}, u32[]{:S(2)}) collective-permute-start(f32[8,128]{1,0:T(8,128)S(1)} %add_add_fusion.2), channel_id=1, source_target_pairs={{0,16},{1,17},{2,18},{3,19},{4,20},{5,21},{6,22},{7,23},{8,24},{9,... | collective-permute-start | bytes 12296 | tf_op jit(solution)/shard_map/ppermute | solution.py:286
  110.4 4.5 %collective-permute-start.28 = (f32[8,128]{1,0:T(8,128)S(1)}, f32[8,128]{1,0:T(8,128)S(1)}, u32[]{:S(2)}, u32[]{:S(2)}) collective-permute-start(f32[8,128]{1,0:T(8,128)S(1)} %add_add_fusion.1), channel_id=1, source_target_pairs={{0,96},{1,97},{2,98},{3,99},{4,100},{5,101},{6,102},{7,103},{8,104... | collective-permute-start | bytes 12296 | tf_op jit(solution)/shard_map/ppermute | solution.py:286
  113.4 4.8 %collective-permute-start.27 = (f32[8,128]{1,0:T(8,128)S(1)}, f32[8,128]{1,0:T(8,128)S(1)}, u32[]{:S(2)}, u32[]{:S(2)}) collective-permute-start(f32[8,128]{1,0:T(8,128)S(1)} %add_add_fusion.1), channel_id=1, source_target_pairs={{0,32},{1,33},{2,34},{3,35},{4,36},{5,37},{6,38},{7,39},{8,40},{9,... | collective-permute-start | bytes 12296 | tf_op jit(solution)/shard_map/ppermute | solution.py:286
  113.4 5.1 %collective-permute-start.26 = (f32[8,128]{1,0:T(8,128)S(1)}, f32[8,128]{1,0:T(8,128)S(1)}, u32[]{:S(2)}, u32[]{:S(2)}) collective-permute-start(f32[8,128]{1,0:T(8,128)S(1)} %add_add_fusion.1), channel_id=1, source_target_pairs={{0,64},{1,65},{2,66},{3,67},{4,68},{5,69},{6,70},{7,71},{8,72},{9,... | collective-permute-start | bytes 12296 | tf_op jit(solution)/shard_map/ppermute | solution.py:286
